TPU v7x, 128 devices: a whole 4x4x4 slice. The times are simulated.
128 devices in a mesh: line: 8 (over x_hi, z), out: 16 (over x_lo, y, core).
Axes of the slice: x: 4 (x_hi: 2, x_lo: 2; x = x_hi * 2 + x_lo), y: 4, z: 4, core: 2. Of those that a mesh axis runs over, the one named last changes fastest.
Arguments:
- injections: bfloat16 [32, 8192], P(None, 'out'), may hold values from -6 to 6
- shift_factors: bfloat16 [16384, 8192], P('line', 'out'), may hold values from -0.0625 to 0.0625
- outage_factors: bfloat16 [16384, 16384], P('out', 'line'), may hold values from -3 to 3
- limits: float32 [16384], P('line'), may hold values from 0.6 to 1.6
- outage_line: int32 [16384], P('out'), may hold values from 0 to 16383, each once
- tile_list: int32 [16, 16], P('out'), may hold values from 0 to 15, as said below
- tile_count: int32 [16], P('out'), may hold values from 1 to 16, as said below
Outputs:
- injection_grad: float32 [32, 8192], P(None, 'out')
Inputs may be any that keep to these rules, and one draw needn't show every extreme that they name: `outage_line`: each line is taken out by exactly one outage. `tile_list`: each row names every one of its 16 local tiles once, in an order drawn from the seed. `tile_count`: some index of out has all its tiles screened in.
All inputs are finite; a program needn't handle non-finite values.
Results may differ from a plain program's by a relative error of at most 0.0018.
Values may be sent and summed in bfloat16 or wider, within the bound.
A program may use at most 64 MiB of HBM per device.

v0:
```python
import jax
import jax.numpy as jnp
from jax import lax
from jax.sharding import PartitionSpec as P

NL = 16384
TILE = 64
NO = 16384


def dense_terms(direct, reverse, outage_line, line_start, line_dev):
    cases = direct.shape[0]
    grad_terms = jnp.zeros((cases, NL), jnp.float32).at[:, outage_line].add(reverse)
    own_terms = lax.dynamic_slice_in_dim(grad_terms, line_start, line_dev, 1) + direct
    return lax.dynamic_update_slice_in_dim(grad_terms, own_terms, line_start, 1)


def shards(injections, shift_factors, outage_factors, limits, outage_line, tile_list, tile_count):
    cases = injections.shape[0]
    line_dev = shift_factors.shape[0]
    out_dev = outage_factors.shape[0]
    partial_flows = lax.dot_general(
        injections, shift_factors, (((1,), (1,)), ((), ())), preferred_element_type=jnp.float32
    )
    line_flows = lax.psum(partial_flows, "out")
    line_start = lax.axis_index("line") * line_dev
    all_flows = lax.all_gather(line_flows, "line", axis=1, tiled=True)
    fall_flows = jnp.take(all_flows, outage_line, axis=1)
    weight_scale = 2.0 / NO
    listing = tile_list[0]

    def tile_step(loop_step, carried):
        direct, reverse = carried
        tile_start = listing[loop_step] * TILE
        factors_wide = lax.dynamic_slice_in_dim(outage_factors, tile_start, TILE, 0).astype(
            jnp.float32
        )
        fallen_block = lax.dynamic_slice_in_dim(fall_flows, tile_start, TILE, 1)
        post_flow = line_flows[:, None, :] + fallen_block[:, :, None] * factors_wide[None]
        excess = jnp.maximum(jnp.abs(post_flow) - limits[None, None, :], 0.0)
        slope = weight_scale * excess * jnp.sign(post_flow)
        direct = direct + jnp.sum(slope, axis=1)
        reverse = lax.dynamic_update_slice_in_dim(
            reverse, jnp.sum(slope * factors_wide[None], axis=2), tile_start, 1
        )
        return (direct, reverse)

    start_state = (
        jnp.zeros((cases, line_dev), jnp.float32),
        jnp.zeros((cases, out_dev), jnp.float32),
    )
    direct, reverse = lax.fori_loop(0, tile_count[0], tile_step, start_state)
    grad_terms = dense_terms(direct, reverse, outage_line, line_start, line_dev)
    grad_piece = lax.psum_scatter(grad_terms, ("line", "out"), scatter_dimension=1, tiled=True)
    grad_round = lax.all_gather(grad_piece.astype(jnp.bfloat16), "out", axis=1, tiled=True)
    partial_grad = jnp.dot(grad_round, shift_factors, preferred_element_type=jnp.float32)
    return lax.psum(partial_grad, "line")


def solution(mesh):
    placed = (
        P(None, "out"),
        P("line", "out"),
        P("out", "line"),
        P("line"),
        P("out"),
        P("out", None),
        P("out"),
    )
    return jax.shard_map(
        shards, mesh=mesh, in_specs=placed, out_specs=P(None, "out"), check_vma=False
    )
```

profile of v0, /device:TPU:0, one launch (start us, length us, event | category | flops | bytes accessed | tf_op | source)
XLA Modules:
  0.0 1217.2 jit_solution(2287972033138165834)
XLA Ops:
  6.5 1.6 copy-done
  8.1 2.2 fusion.3
  10.4 119.0 %all-reduce.3.cloned.1.call-done = f32[32,2048]{1,0:T(8,128)} async-done(((f32[32,2048]{1,0:T(8,128)}), f32[32,2048]{1,0:T(8,128)}) %all-reduce.3.cloned.1.call-update) | async-done | bytes 262160 | tf_op jit(solution)/shard_map/psum | solution.py:25
  130.8 56.4 %all-gather.2.cloned.1.call-done = f32[32,16384]{1,0:T(8,128)} async-done(((f32[32,2048]{1,0:T(8,128)}), f32[32,16384]{1,0:T(8,128)}) %all-gather.2.cloned.1.call-update) | async-done | bytes 2097168 | tf_op jit(solution)/shard_map/all_gather | solution.py:27
  187.2 6.2 copy.12
  193.5 7.4 gather_fusion
  200.9 1.2 select_bitcast_fusion
  202.4 92.6 %while.12 = (s32[]{:T(128)}, f32[32,2048]{1,0:T(8,128)S(1)}, f32[32,1024]{1,0:T(8,128)S(1)}, s32[]{:T(128)}, f32[32,2048]{1,0:T(8,128)S(1)}, /*index=5*/s32[16]{...) while((s32[]{:T(128)}, f32[32,2048]{1,0:T(8,128)S(1)}, ...), condition=%wide.region_4.5_spmd, body=%wide.region_1.4_spmd.sunk | while | flops 46266376 | bytes 2679029 | solution.py:52
  204.4 1.0 dynamic-slice_convert_fusion.2
  205.3 11.9 multiply_reduce_fusion.2
  219.7 1.0 dynamic-slice_convert_fusion.2
  220.7 11.9 multiply_reduce_fusion.2
  236.0 11.9 multiply_reduce_fusion.2
  251.4 11.9 multiply_reduce_fusion.2
  266.7 11.9 multiply_reduce_fusion.2
  281.9 11.9 multiply_reduce_fusion.2
  295.0 1.1 copy.14
  296.4 10.1 scatter_custom_fusion
  306.5 2.3 add_dynamic-update-slice_fusion
  308.9 801.9 %reduce-scatter.2.cloned.1.call-done = f32[32,128]{0,1:T(8,128)} async-done(((f32[32,16384]{0,1:T(8,128)}), f32[32,128]{0,1:T(8,128)}) %reduce-scatter.2.cloned.1.call-update) | async-done | bytes 16400 | tf_op jit(solution)/shard_map/reduce_scatter | solution.py:54
  1111.7 17.5 %all_gather.7 = bf16[32,2048]{0,1:T(8,128)(2,1)S(1)} all-gather(bf16[32,128]{0,1:T(8,128)(2,1)S(1)} %convert_element_type.6), channel_id=1, replica_groups=mesh['line'=8,'out'=16] {'out'}, dimensions={1}, use_global_device_ids=true | all-gather | bytes 139264 | tf_op jit(solution)/shard_map/all_gather | solution.py:55
  1129.2 1.1 fusion.4
  1130.3 78.9 %all-reduce.5.cloned.1.call-done = f32[32,512]{1,0:T(8,128)} async-done(((f32[32,512]{1,0:T(8,128)}), f32[32,512]{1,0:T(8,128)}) %all-reduce.5.cloned.1.call-update) | async-done | bytes 65552 | tf_op jit(solution)/shard_map/psum | solution.py:57
  1209.2 1.5 copy.29
  (50 shorter events, 13.8 us)
Async XLA Ops:
  6.5 1.6 copy-start
  6.5 195.8 %copy-start.3 = (s32[1,16]{1,0:T(1,128)S(1)}, s32[1,16]{1,0:T(1,128)}, u32[]{:S(2)}) copy-start(s32[1,16]{1,0:T(1,128)} %param.14) | copy-start | bytes 196
  6.5 195.8 %copy-start.2 = (f32[2048]{0:T(1024)S(1)}, f32[2048]{0:T(1024)}, u32[]{:S(2)}) copy-start(f32[2048]{0:T(1024)} %param.12) | copy-start | bytes 24580
  6.5 122.8 %all-reduce.3.cloned.1.call-start = ((), (), s32[]{:S(2)}) async-start(), calls=%async_computation.1 | async-start | bytes 524288 | tf_op jit(solution)/shard_map/psum | solution.py:25
  10.3 176.9 %all-gather.2.cloned.1.call-start = ((), (), s32[]{:S(2)}) async-start(), calls=%async_computation.2 | async-start | bytes 2359296 | tf_op jit(solution)/shard_map/all_gather | solution.py:27
  129.3 73.0 %copy-start.1 = (f32[32,2048]{1,0:T(8,128)S(1)}, f32[32,2048]{1,0:T(8,128)}, u32[]{:S(2)}) copy-start(f32[32,2048]{1,0:T(8,128)} %all-reduce.3.cloned.1.call-done) | copy-start | bytes 786436
  129.4 981.5 %reduce-scatter.2.cloned.1.call-start = ((), (), s32[]{:S(2)}) async-start(), calls=%async_computation.3 | async-start | bytes 8454144 | tf_op jit(solution)/shard_map/reduce_scatter | solution.py:54
  308.8 900.3 %all-reduce.5.cloned.1.call-start = ((), (), s32[]{:S(2)}) async-start(), calls=%async_computation.4 | async-start | bytes 131072 | tf_op jit(solution)/shard_map/psum | solution.py:57
Sparse Core Ops, SparseCore 0:
  10.4 118.8 all-reduce.2
  131.9 55.2 all-gather.1
  309.0 801.8 reduce-scatter.1
  1130.4 78.6 all-reduce.4
where the time goes:
time: 1220 us
  waiting for transfers between devices  1060 us (87%)
  other arithmetic  93.4 us (8%)
  local copies, waits for them, and re-layouts  24.8 us (2%)
  blocking collectives  17.5 us (1%)
  between operations  13.2 us (1%)
    reduce_scatter x1, waiting for transfers between devices, shards(): lax.psum_scatter(grad_terms, ('line', 'out'), scatter_dimension=1, tiled=...  802 us
    psum x1, waiting for transfers between devices, shards(): line_flows = lax.psum(partial_flows, 'out')  119 us
    psum x1, waiting for transfers between devices, shards(): return lax.psum(partial_grad, 'line')  78.9 us
    reduce_sum x6, other arithmetic, tile_step(): jnp.sum(slope * factors_wide[None], axis=2)  71.2 us
    all_gather x1, waiting for transfers between devices, shards(): all_flows = lax.all_gather(line_flows, 'line', axis=1, tiled=True)  56.4 us
  transfers between devices with their start and end apart: 4, of which 4 were waited for; matrix products, arithmetic and copies ran while one was open for 0% of the time, Pallas kernels for 0%

commit v1 on v0

v1 whole, which is shorter than its diff:
```python
import functools

import jax
import jax.numpy as jnp
from jax import lax
from jax.experimental import pallas as pl
from jax.experimental.pallas import tpu as pltpu
from jax.sharding import PartitionSpec as P

CASES = 32
NO = 16384
TILE = 64
LB = 128
F32 = jnp.float32
BF16 = jnp.bfloat16
MESH = pl.DeviceIdType.MESH
VMEM = pl.BlockSpec(memory_space=pltpu.VMEM)
SMEM = pl.BlockSpec(memory_space=pltpu.SMEM)


def peer(axis, size, offset):
    if axis == "out":
        return (lax.axis_index("line"), lax.rem(lax.axis_index("out") + offset, size))
    return (lax.rem(lax.axis_index("line") + offset, size), lax.axis_index("out"))


def greet(n_line, n_out):
    barrier = pltpu.get_barrier_semaphore()
    for i in range(1, n_out):
        pl.semaphore_signal(barrier, inc=1, device_id=peer("out", n_out, i), device_id_type=MESH)
    for i in range(1, n_line):
        pl.semaphore_signal(barrier, inc=1, device_id=peer("line", n_line, i), device_id_type=MESH)
    return barrier


def send(src, dst, sems, i, axis, size):
    copy = pltpu.make_async_remote_copy(
        src_ref=src,
        dst_ref=dst,
        send_sem=sems.at[0, i],
        recv_sem=sems.at[1, i],
        device_id=peer(axis, size, i),
        device_id_type=MESH,
    )
    copy.start()
    return copy


def split3(x):
    hi = x.astype(BF16)
    rest = x - hi.astype(F32)
    mid = rest.astype(BF16)
    low = (rest - mid.astype(F32)).astype(BF16)
    return jnp.concatenate([hi, mid, low], axis=0)


def scatter_sum(parts, recv, sems, axis, size, fill=None):
    me = lax.axis_index(axis)
    copies = []
    for i in range(1, size):
        d = lax.rem(me + i, size)
        if fill is not None:
            fill(d)
        copies.append(send(parts.at[d], recv.at[i], sems, i, axis, size))
    if fill is not None:
        fill(me)
    total = parts[me]
    for i in range(1, size):
        copies[i - 1].wait_recv()
        total = total + recv[i]
    for copy in copies:
        copy.wait_send()
    return total


def spread(slots, sems, axis, size):
    me = lax.axis_index(axis)
    copies = [send(slots.at[me], slots.at[me], sems, i, axis, size) for i in range(1, size)]
    for copy in copies:
        copy.wait_recv()
    for copy in copies:
        copy.wait_send()


def flows_kernel(
    n_line, n_out, inj_ref, sf_ref, line_ref, lf_ref, ff_ref,
    parts, recv_o, slots_o, hot, picked, recv_l, slots_l, s_ro, s_go, s_rl, s_gl,
):
    barrier = greet(n_line, n_out)
    line_start = lax.axis_index("line") * (n_out * LB)
    n_k = n_line * LB

    def fill(d):
        rows = sf_ref[pl.ds(pl.multiple_of(d * LB, LB), LB), :]
        parts[d] = lax.dot_general(
            inj_ref[...], rows, (((1,), (1,)), ((), ())), preferred_element_type=F32
        )

    pl.semaphore_wait(barrier, n_out + n_line - 2)
    me_out = lax.axis_index("out")
    me_line = lax.axis_index("line")
    copies = []
    for i in range(1, n_out):
        d = lax.rem(me_out + i, n_out)
        fill(d)
        copies.append(send(parts.at[d], recv_o.at[i], s_ro, i, "out", n_out))
    fill(me_out)
    local = line_ref[...] - line_start

    def hot_rows(r, _):
        base = pl.multiple_of(r * LB, LB)
        ids = lax.broadcasted_iota(jnp.int32, (LB, n_k), 0) + base
        hot[pl.ds(base, LB), :] = (ids == local).astype(F32).astype(BF16)
        return 0

    lax.fori_loop(0, n_out, hot_rows, 0)
    total = parts[me_out]
    for i in range(1, n_out):
        copies[i - 1].wait_recv()
        total = total + recv_o[i]
    slots_o[me_out] = total
    spread(slots_o, s_go, "out", n_out)
    for copy in copies:
        copy.wait_send()
    lf_ref[...] = slots_o[...]

    wide = jnp.concatenate([slots_o[i] for i in range(n_out)], axis=1)
    got = jnp.dot(split3(wide), hot[...], preferred_element_type=F32)
    got = got[:CASES] + got[CASES : 2 * CASES] + got[2 * CASES :]
    for i in range(n_line):
        picked[i] = got[:, i * LB : (i + 1) * LB]
    slots_l[me_line] = scatter_sum(picked, recv_l, s_rl, "line", n_line)
    spread(slots_l, s_gl, "line", n_line)
    ff_ref[...] = slots_l[...]


def flows(n_line, n_out, injections, shift_factors, outage_line):
    n_k = n_line * LB
    block = (CASES, LB)
    dma = pltpu.SemaphoreType.DMA
    return pl.pallas_call(
        functools.partial(flows_kernel, n_line, n_out),
        in_specs=[VMEM, VMEM, VMEM],
        out_specs=[VMEM, VMEM],
        out_shape=[
            jax.ShapeDtypeStruct((n_out,) + block, F32),
            jax.ShapeDtypeStruct((n_line,) + block, F32),
        ],
        scratch_shapes=[
            pltpu.VMEM((n_out,) + block, F32),
            pltpu.VMEM((n_out,) + block, F32),
            pltpu.VMEM((n_out,) + block, F32),
            pltpu.VMEM((n_out * LB, n_k), BF16),
            pltpu.VMEM((n_line,) + block, F32),
            pltpu.VMEM((n_line,) + block, F32),
            pltpu.VMEM((n_line,) + block, F32),
            dma((2, n_out)),
            dma((2, n_out)),
            dma((2, n_line)),
            dma((2, n_line)),
        ],
        compiler_params=pltpu.CompilerParams(
            collective_id=0, has_side_effects=True, vmem_limit_bytes=40 * 2**20
        ),
        name="flows",
    )(injections, shift_factors, outage_line.reshape(1, n_k))


def terms_kernel(
    n_line, n_out, list_ref, count_ref, of_ref, lf_ref, lim_ref, ff_ref, dir_ref, rev_ref,
    wide_of, low, high, fall, dsum, qsum, rtile,
):
    n_l = n_out * LB
    for t in range(n_out):
        cols = pl.ds(t * LB, LB)
        lim = lim_ref[:, cols]
        flow = lf_ref[t]
        for c in range(CASES):
            low[c, :, cols] = jnp.broadcast_to(-lim - flow[c : c + 1], (8, LB))
            high[c, :, cols] = jnp.broadcast_to(lim - flow[c : c + 1], (8, LB))
    dsum[...] = jnp.zeros_like(dsum)
    qsum[...] = jnp.zeros_like(qsum)
    rtile[...] = jnp.zeros_like(rtile)

    def fall_block(kb, _):
        turned = ff_ref[kb].T
        rows = pl.ds(pl.multiple_of(kb * LB, LB), LB)
        for c in range(CASES):
            fall[c, rows, :] = jnp.broadcast_to(turned[:, c : c + 1], (LB, LB))
        return 0

    lax.fori_loop(0, n_line, fall_block, 0)
    ones = jnp.ones((8, LB), F32)

    def tile_step(step, _):
        tile = list_ref[0, step]
        k0 = pl.multiple_of(tile * TILE, TILE)
        narrow = of_ref[pl.ds(k0, TILE), :]
        wide_of[...] = narrow.astype(F32)
        pair = ff_ref[tile // 2]
        half = lax.rem(tile, 2) == 0
        mine = jnp.where(half, pair[:, :TILE], pair[:, TILE:])
        prod = jnp.dot(split3(mine), narrow, preferred_element_type=F32)
        qsum[...] += prod[:CASES] + prod[CASES : 2 * CASES] + prod[2 * CASES :]
        square = jnp.zeros((TILE, LB), F32)
        for t in range(n_out):
            w = wide_of[:, t * LB : (t + 1) * LB]
            square = square + w * w

        def case_step(c, _):
            ffs = [fall[c, pl.ds(k0 + 8 * i, 8), :] for i in range(TILE // 8)]
            acc = [ffs[i] * square[8 * i : 8 * i + 8] for i in range(TILE // 8)]
            for t in range(n_out):
                cols = pl.ds(t * LB, LB)
                lo = low[c, :, cols]
                hi = high[c, :, cols]
                total = None
                for i in range(TILE // 8):
                    o = wide_of[8 * i : 8 * i + 8, t * LB : (t + 1) * LB]
                    q = jnp.minimum(jnp.maximum(ffs[i] * o, lo), hi)
                    acc[i] = acc[i] - q * o
                    total = q if total is None else total + q
                dsum[c, :, cols] += total
            row = lax.dot_general(
                ones, jnp.concatenate(acc, axis=0), (((1,), (1,)), ((), ())),
                precision=lax.Precision.HIGHEST, preferred_element_type=F32,
            )
            rtile[tile, pl.ds(c, 1), 0:TILE] = row[0:1]
            return 0

        lax.fori_loop(0, CASES, case_step, 0)
        return 0

    lax.fori_loop(0, count_ref[0], tile_step, 0)
    for t in range(n_out):
        cols = slice(t * LB, (t + 1) * LB)
        dir_ref[t] = qsum[:, cols] - jnp.sum(dsum[:, :, cols], axis=1)
    for b in range(n_line):
        rev_ref[b] = jnp.concatenate([rtile[2 * b, :, :TILE], rtile[2 * b + 1, :, :TILE]], axis=1)


def terms(n_line, n_out, tile_list, tile_count, outage_factors, lf, limits, ff):
    n_l = n_out * LB
    n_k = n_line * LB
    block = (CASES, LB)
    return pl.pallas_call(
        functools.partial(terms_kernel, n_line, n_out),
        in_specs=[SMEM, SMEM, VMEM, VMEM, VMEM, VMEM],
        out_specs=[VMEM, VMEM],
        out_shape=[
            jax.ShapeDtypeStruct((n_out,) + block, F32),
            jax.ShapeDtypeStruct((n_line,) + block, F32),
        ],
        scratch_shapes=[
            pltpu.VMEM((TILE, n_l), F32),
            pltpu.VMEM((CASES, 8, n_l), F32),
            pltpu.VMEM((CASES, 8, n_l), F32),
            pltpu.VMEM((CASES, n_k, LB), F32),
            pltpu.VMEM((CASES, 8, n_l), F32),
            pltpu.VMEM((CASES, n_l), F32),
            pltpu.VMEM((n_k // TILE, CASES, LB), F32),
        ],
        compiler_params=pltpu.CompilerParams(vmem_limit_bytes=56 * 2**20),
        name="terms",
    )(tile_list, tile_count, outage_factors, lf, limits.reshape(1, n_l), ff)


def grads_kernel(
    n_line, n_out, dir_ref, rev_ref, line_ref, sf_ref, out_ref,
    recv_r, slots_r, hot, parts, recv_o, slots_o, shares, recv_f, slots_f,
    s_rr, s_gr, s_ro, s_go, s_rf, s_gf,
):
    barrier = greet(n_line, n_out)
    me_line = lax.axis_index("line")
    me_out = lax.axis_index("out")
    line_start = me_line * (n_out * LB)
    n_k = n_line * LB
    pl.semaphore_wait(barrier, n_out + n_line - 2)
    copies = []
    for i in range(1, n_line):
        d = lax.rem(me_line + i, n_line)
        copies.append(send(rev_ref.at[d], recv_r.at[i], s_rr, i, "line", n_line))
    local = line_ref[...] - line_start

    def hot_rows(r, _):
        base = pl.multiple_of(r * LB, LB)
        ids = lax.broadcasted_iota(jnp.int32, (LB, n_k), 0) + base
        hot[pl.ds(base, LB), :] = (ids == local).astype(F32).astype(BF16)
        return 0

    lax.fori_loop(0, n_out, hot_rows, 0)
    total = rev_ref[me_line]
    for i in range(1, n_line):
        copies[i - 1].wait_recv()
        total = total + recv_r[i]
    slots_r[me_line] = total
    spread(slots_r, s_gr, "line", n_line)
    for copy in copies:
        copy.wait_send()
    three = split3(jnp.concatenate([slots_r[i] for i in range(n_line)], axis=1))

    def fill(d):
        table = hot[pl.ds(pl.multiple_of(d * LB, LB), LB), :]
        got = lax.dot_general(three, table, (((1,), (1,)), ((), ())), preferred_element_type=F32)
        parts[d] = dir_ref[d] + (got[:CASES] + got[CASES : 2 * CASES] + got[2 * CASES :])

    grad = scatter_sum(parts, recv_o, s_ro, "out", n_out, fill)
    slots_o[me_out] = (grad * (2.0 / NO)).astype(BF16)
    spread(slots_o, s_go, "out", n_out)
    rounded = jnp.concatenate([slots_o[i] for i in range(n_out)], axis=1)
    partial = jnp.dot(rounded, sf_ref[...], preferred_element_type=F32)
    half = CASES // 2
    for i in range(n_line):
        r, q = i % 2, i // 2
        shares[i] = partial[r * half : (r + 1) * half, q * LB : (q + 1) * LB]
    slots_f[me_line] = scatter_sum(shares, recv_f, s_rf, "line", n_line)
    spread(slots_f, s_gf, "line", n_line)
    for i in range(n_line):
        r, q = i % 2, i // 2
        out_ref[r * half : (r + 1) * half, q * LB : (q + 1) * LB] = slots_f[i]


def grads(n_line, n_out, direct, reverse, outage_line, shift_factors):
    n_k = n_line * LB
    block = (CASES, LB)
    share = (n_line, CASES // 2, LB)
    dma = pltpu.SemaphoreType.DMA
    return pl.pallas_call(
        functools.partial(grads_kernel, n_line, n_out),
        in_specs=[VMEM] * 4,
        out_specs=VMEM,
        out_shape=jax.ShapeDtypeStruct((CASES, shift_factors.shape[1]), F32),
        scratch_shapes=[
            pltpu.VMEM((n_line,) + block, F32),
            pltpu.VMEM((n_line,) + block, F32),
            pltpu.VMEM((n_out * LB, n_k), BF16),
            pltpu.VMEM((n_out,) + block, F32),
            pltpu.VMEM((n_out,) + block, F32),
            pltpu.VMEM((n_out,) + block, BF16),
            pltpu.VMEM(share, F32),
            pltpu.VMEM(share, F32),
            pltpu.VMEM(share, F32),
            dma((2, n_line)),
            dma((2, n_line)),
            dma((2, n_out)),
            dma((2, n_out)),
            dma((2, n_line)),
            dma((2, n_line)),
        ],
        compiler_params=pltpu.CompilerParams(
            collective_id=1, has_side_effects=True, vmem_limit_bytes=40 * 2**20
        ),
        name="grads",
    )(direct, reverse, outage_line.reshape(1, n_k), shift_factors)


def shards(
    n_line, n_out, injections, shift_factors, outage_factors, limits, outage_line, tile_list, tile_count
):
    lf, ff = flows(n_line, n_out, injections, shift_factors, outage_line)
    direct, reverse = terms(n_line, n_out, tile_list, tile_count, outage_factors, lf, limits, ff)
    return grads(n_line, n_out, direct, reverse, outage_line, shift_factors)


def solution(mesh):
    placed = (
        P(None, "out"),
        P("line", "out"),
        P("out", "line"),
        P("line"),
        P("out"),
        P("out", None),
        P("out"),
    )
    return jax.shard_map(
        functools.partial(shards, mesh.shape["line"], mesh.shape["out"]),
        mesh=mesh,
        in_specs=placed,
        out_specs=P(None, "out"),
        check_vma=False,
    )
```

time: 1220 us -> 221 us (0.18)
  waiting for transfers between devices: 1060 us -> 0 us
  Pallas kernels: 0 us -> 213 us
  other arithmetic: 93.4 us -> 0 us
  local copies, waits for them, and re-layouts: 24.8 us -> 6.86 us
  blocking collectives: 17.5 us -> 0 us
  between operations: 13.2 us -> 0.71 us
    reduce_scatter x1 -> x0, waiting for transfers between devices: 802 us -> none  [shards(): lax.psum_scatter(grad_terms, ('line', 'out'), scatter_dimension=1, tiled=...]
    pallas_call x0 -> x3, Pallas kernels: none -> 213 us  [the longest x1 107 us: terms(): pl.pallas_call(functools.partial(terms_kernel, n_line, n_out), in_specs=[...]
    psum x2 -> x0, waiting for transfers between devices: 198 us -> none  [the longest x1 119 us: shards(): line_flows = lax.psum(partial_flows, 'out')]
    reduce_sum x6 -> x0, other arithmetic: 71.2 us -> none  [tile_step(): jnp.sum(slope * factors_wide[None], axis=2)]
    all_gather x1 -> x0, waiting for transfers between devices: 56.4 us -> none  [shards(): all_flows = lax.all_gather(line_flows, 'line', axis=1, tiled=True)]
    all_gather x1 -> x0, blocking collectives: 17.5 us -> none  [shards(): lax.all_gather(grad_piece.astype(jnp.bfloat16), 'out', axis=1, tiled=True)]
  transfers between devices with their start and end apart: 4 -> 0, of which waited for: 4 -> 0; matrix products, arithmetic and copies ran while one was open for 0% -> 0% of each run, Pallas kernels for 0% -> 0%
where the time goes in v1:
time: 221 us
  Pallas kernels  213 us (96%)
  local copies, waits for them, and re-layouts  6.86 us (3%)
    pallas_call x1, Pallas kernels, terms(): pl.pallas_call(functools.partial(terms_kernel, n_line, n_out), in_specs=[...  107 us
    pallas_call x1, Pallas kernels, grads(): pl.pallas_call(functools.partial(grads_kernel, n_line, n_out), in_specs=[...  76 us
    pallas_call x1, Pallas kernels, flows(): pl.pallas_call(functools.partial(flows_kernel, n_line, n_out), in_specs=[...  30.5 us
    unnamed x19, local copies, waits for them, and re-layouts  6.86 us

profile of v1, /device:TPU:0, one launch (start us, length us, event | category | flops | bytes accessed | tf_op | source)
XLA Modules:
  0.0 220.7 jit_solution(13287217659329738863)
XLA Ops:
  0.0 0.0 copy-start.8
  0.7 0.0 copy-start
  0.7 1.6 copy-done
  2.3 0.0 copy-start.6
  2.3 0.8 copy-done.6
  3.0 0.0 copy-start.7
  3.0 0.7 copy-done.7
  3.7 0.0 copy-start.1
  3.7 30.5 %flows.1 = (f32[16,32,128]{2,1,0:T(8,128)S(1)}, f32[8,32,128]{2,1,0:T(8,128)S(1)}) custom-call(bf16[32,512]{1,0:T(8,128)(2,1)S(1)} %copy-done.6, bf16[2048,512]{1,0:T(8,128)(2,1)S(1)} %copy-done, s32[1,1024]{1,0:T(1,128)S(1)} %bitcast.2), custom_call_target="tpu_custom_call" | custom-call | tf_op jit(solution)/shard_map/flows/pallas_call | solution.py:141
  34.2 0.0 copy-start.2
  34.2 0.7 copy-done.2
  34.9 0.0 copy-start.4
  35.0 0.6 copy-done.4
  35.6 106.6 %terms.1 = (f32[16,32,128]{2,1,0:T(8,128)}, f32[8,32,128]{2,1,0:T(8,128)}) custom-call(s32[1,16]{1,0:T(1,128)} %list_ref.1, s32[1]{0:T(128)S(6)} %copy.9.count_ref, bf16[1024,2048]{1,0:T(8,128)(2,1)} %of_ref.1, f32[16,32,128]{2,1,0:T(8,128)} %copy-done.2, f32[1,2048]{1,0:T(1,128)} %bitcast.4, f32[8,32,128]{2,1,0:T(8,128)} %copy-done.4), custom_call_target="tpu_custom_call" | custom-call | tf_op jit(solution)/shard_map/terms/pallas_call | solution.py:246
  142.2 0.0 copy-done.8
  142.2 0.0 copy-done.1
  142.2 0.0 copy-start.3
  142.2 0.9 copy-done.3
  143.2 0.0 copy-start.5
  143.2 0.9 copy-done.5
  144.1 76.0 %grads.1 = f32[32,512]{1,0:T(8,128)S(1)} custom-call(f32[16,32,128]{2,1,0:T(8,128)S(1)} %copy-done.3, f32[8,32,128]{2,1,0:T(8,128)S(1)} %copy-done.5, s32[1,1024]{1,0:T(1,128)S(1)} %bitcast.3, bf16[2048,512]{1,0:T(8,128)(2,1)S(1)} %copy-done.1), custom_call_target="tpu_custom_call" | custom-call | tf_op jit(solution)/shard_map/grads/pallas_call | solution.py:328
  220.1 0.6 copy.10
Async XLA Ops:
  0.0 142.2 %copy-start.8 = (s32[1024]{0:T(1024)S(1)}, s32[1024]{0:T(1024)}, u32[]{:S(2)}) copy-start(s32[1024]{0:T(1024)} %param.11) | copy-start | bytes 12292
  0.7 1.6 copy-start
  2.3 0.8 copy-start.6
  3.0 0.7 copy-start.7
  3.7 138.5 %copy-start.1 = (bf16[2048,512]{1,0:T(8,128)(2,1)S(1)}, bf16[2048,512]{1,0:T(8,128)(2,1)}, u32[]{:S(2)}) copy-start(bf16[2048,512]{1,0:T(8,128)(2,1)} %sf_ref.3) | copy-start | bytes 6291460
  34.2 0.7 copy-start.2
  34.9 0.6 copy-start.4
  142.2 1.0 copy-start.3
  143.2 0.9 copy-start.5

commit v2 on v1

--- a/solution.py
+++ b/solution.py
@@ -168,9 +168,8 @@
 
 def terms_kernel(
     n_line, n_out, list_ref, count_ref, of_ref, lf_ref, lim_ref, ff_ref, dir_ref, rev_ref,
-    wide_of, low, high, fall, dsum, qsum, rtile,
+    wide_of, low, high, fall, dsum, qsum, turned, rsum,
 ):
-    n_l = n_out * LB
     for t in range(n_out):
         cols = pl.ds(t * LB, LB)
         lim = lim_ref[:, cols]
@@ -178,19 +177,13 @@
         for c in range(CASES):
             low[c, :, cols] = jnp.broadcast_to(-lim - flow[c : c + 1], (8, LB))
             high[c, :, cols] = jnp.broadcast_to(lim - flow[c : c + 1], (8, LB))
+    for b in range(n_line):
+        turned[b * LB : (b + 1) * LB, 0:CASES] = ff_ref[b].T
     dsum[...] = jnp.zeros_like(dsum)
     qsum[...] = jnp.zeros_like(qsum)
-    rtile[...] = jnp.zeros_like(rtile)
-
-    def fall_block(kb, _):
-        turned = ff_ref[kb].T
-        rows = pl.ds(pl.multiple_of(kb * LB, LB), LB)
-        for c in range(CASES):
-            fall[c, rows, :] = jnp.broadcast_to(turned[:, c : c + 1], (LB, LB))
-        return 0
-
-    lax.fori_loop(0, n_line, fall_block, 0)
-    ones = jnp.ones((8, LB), F32)
+    rsum[...] = jnp.zeros_like(rsum)
+    n_sub = TILE // 8
+    lanes = lax.broadcasted_iota(jnp.int32, (8, LB), 1)
 
     def tile_step(step, _):
         tile = list_ref[0, step]
@@ -206,29 +199,39 @@
         for t in range(n_out):
             w = wide_of[:, t * LB : (t + 1) * LB]
             square = square + w * w
-
-        def case_step(c, _):
-            ffs = [fall[c, pl.ds(k0 + 8 * i, 8), :] for i in range(TILE // 8)]
-            acc = [ffs[i] * square[8 * i : 8 * i + 8] for i in range(TILE // 8)]
+        for c in range(CASES):
+            fall[c] = jnp.broadcast_to(turned[pl.ds(k0, TILE), c : c + 1], (TILE, LB))
+
+        def reduce_rows(c, sums):
+            return tuple(
+                jnp.where(lanes == c, jnp.sum(fall[jnp.maximum(c, 0), 8 * i : 8 * i + 8, :], axis=1, keepdims=True), sums[i])
+                for i in range(n_sub)
+            )
+
+        def case_step(c, sums):
+            sums = reduce_rows(c - 1, sums)
+            ffs = [fall[c, 8 * i : 8 * i + 8, :] for i in range(n_sub)]
+            acc = [ffs[i] * square[8 * i : 8 * i + 8] for i in range(n_sub)]
             for t in range(n_out):
                 cols = pl.ds(t * LB, LB)
                 lo = low[c, :, cols]
                 hi = high[c, :, cols]
                 total = None
-                for i in range(TILE // 8):
+                for i in range(n_sub):
                     o = wide_of[8 * i : 8 * i + 8, t * LB : (t + 1) * LB]
                     q = jnp.minimum(jnp.maximum(ffs[i] * o, lo), hi)
                     acc[i] = acc[i] - q * o
                     total = q if total is None else total + q
                 dsum[c, :, cols] += total
-            row = lax.dot_general(
-                ones, jnp.concatenate(acc, axis=0), (((1,), (1,)), ((), ())),
-                precision=lax.Precision.HIGHEST, preferred_element_type=F32,
-            )
-            rtile[tile, pl.ds(c, 1), 0:TILE] = row[0:1]
-            return 0
-
-        lax.fori_loop(0, CASES, case_step, 0)
+            for i in range(n_sub):
+                fall[c, 8 * i : 8 * i + 8, :] = acc[i]
+            return sums
+
+        zero = jnp.zeros((8, LB), F32)
+        sums = lax.fori_loop(0, CASES, case_step, (zero,) * n_sub)
+        sums = reduce_rows(CASES - 1, sums)
+        for i in range(n_sub):
+            rsum[pl.ds(k0 + 8 * i, 8), :] = sums[i]
         return 0
 
     lax.fori_loop(0, count_ref[0], tile_step, 0)
@@ -236,7 +239,7 @@
         cols = slice(t * LB, (t + 1) * LB)
         dir_ref[t] = qsum[:, cols] - jnp.sum(dsum[:, :, cols], axis=1)
     for b in range(n_line):
-        rev_ref[b] = jnp.concatenate([rtile[2 * b, :, :TILE], rtile[2 * b + 1, :, :TILE]], axis=1)
+        rev_ref[b] = rsum[b * LB : (b + 1) * LB, :].T[:CASES]
 
 
 def terms(n_line, n_out, tile_list, tile_count, outage_factors, lf, limits, ff):
@@ -255,10 +258,11 @@
             pltpu.VMEM((TILE, n_l), F32),
             pltpu.VMEM((CASES, 8, n_l), F32),
             pltpu.VMEM((CASES, 8, n_l), F32),
-            pltpu.VMEM((CASES, n_k, LB), F32),
+            pltpu.VMEM((CASES, TILE, LB), F32),
             pltpu.VMEM((CASES, 8, n_l), F32),
             pltpu.VMEM((CASES, n_l), F32),
-            pltpu.VMEM((n_k // TILE, CASES, LB), F32),
+            pltpu.VMEM((n_k, LB), F32),
+            pltpu.VMEM((n_k, LB), F32),
         ],
         compiler_params=pltpu.CompilerParams(vmem_limit_bytes=56 * 2**20),
         name="terms",
@@ -267,8 +271,8 @@
 
 def grads_kernel(
     n_line, n_out, dir_ref, rev_ref, line_ref, sf_ref, out_ref,
-    recv_r, slots_r, hot, parts, recv_o, slots_o, shares, recv_f, slots_f,
-    s_rr, s_gr, s_ro, s_go, s_rf, s_gf,
+    recv_r, slots_r, hot, parts, recv_o, slots_o, slots_f,
+    s_rr, s_gr, s_ro, s_go, s_gf,
 ):
     barrier = greet(n_line, n_out)
     me_line = lax.axis_index("line")
@@ -309,21 +313,17 @@
     spread(slots_o, s_go, "out", n_out)
     rounded = jnp.concatenate([slots_o[i] for i in range(n_out)], axis=1)
     partial = jnp.dot(rounded, sf_ref[...], preferred_element_type=F32)
-    half = CASES // 2
-    for i in range(n_line):
-        r, q = i % 2, i // 2
-        shares[i] = partial[r * half : (r + 1) * half, q * LB : (q + 1) * LB]
-    slots_f[me_line] = scatter_sum(shares, recv_f, s_rf, "line", n_line)
+    slots_f[me_line] = partial.astype(BF16)
     spread(slots_f, s_gf, "line", n_line)
-    for i in range(n_line):
-        r, q = i % 2, i // 2
-        out_ref[r * half : (r + 1) * half, q * LB : (q + 1) * LB] = slots_f[i]
+    result = slots_f[0].astype(F32)
+    for i in range(1, n_line):
+        result = result + slots_f[i].astype(F32)
+    out_ref[...] = result
 
 
 def grads(n_line, n_out, direct, reverse, outage_line, shift_factors):
     n_k = n_line * LB
     block = (CASES, LB)
-    share = (n_line, CASES // 2, LB)
     dma = pltpu.SemaphoreType.DMA
     return pl.pallas_call(
         functools.partial(grads_kernel, n_line, n_out),
@@ -337,14 +337,11 @@
             pltpu.VMEM((n_out,) + block, F32),
             pltpu.VMEM((n_out,) + block, F32),
             pltpu.VMEM((n_out,) + block, BF16),
-            pltpu.VMEM(share, F32),
-            pltpu.VMEM(share, F32),
-            pltpu.VMEM(share, F32),
+            pltpu.VMEM((n_line, CASES, shift_factors.shape[1]), BF16),
             dma((2, n_line)),
             dma((2, n_line)),
             dma((2, n_out)),
             dma((2, n_out)),
-            dma((2, n_line)),
             dma((2, n_line)),
         ],
         compiler_params=pltpu.CompilerParams(

time: 221 us -> 139 us (0.63)
  Pallas kernels: 213 us -> 131 us
    pallas_call x1, Pallas kernels: 107 us -> 29.6 us  [terms(): pl.pallas_call(functools.partial(terms_kernel, n_line, n_out), in_specs=[...]
    pallas_call x1, Pallas kernels: 76 us -> 71.1 us  [grads(): pl.pallas_call(functools.partial(grads_kernel, n_line, n_out), in_specs=[...]
where the time goes in v2:
time: 139 us
  Pallas kernels  131 us (94%)
  local copies, waits for them, and re-layouts  6.86 us (5%)
    pallas_call x1, Pallas kernels, grads(): pl.pallas_call(functools.partial(grads_kernel, n_line, n_out), in_specs=[...  71.1 us
    pallas_call x1, Pallas kernels, flows(): pl.pallas_call(functools.partial(flows_kernel, n_line, n_out), in_specs=[...  30.5 us
    pallas_call x1, Pallas kernels, terms(): pl.pallas_call(functools.partial(terms_kernel, n_line, n_out), in_specs=[...  29.6 us
    unnamed x19, local copies, waits for them, and re-layouts  6.86 us

profile of v2, /device:TPU:0, one launch (start us, length us, event | category | flops | bytes accessed | tf_op | source)
XLA Modules:
  0.0 138.8 jit_solution(7544537484896280116)
XLA Ops:
  0.0 0.0 copy-start.8
  0.7 0.0 copy-start
  0.7 1.6 %copy-done = bf16[2048,512]{1,0:T(8,128)(2,1)S(1)} copy-done((bf16[2048,512]{1,0:T(8,128)(2,1)S(1)}, bf16[2048,512]{1,0:T(8,128)(2,1)}, u32[]{:S(2)}) %copy-start) | copy-done | bytes 2097176
  2.3 0.0 copy-start.6
  2.3 0.8 copy-done.6
  3.0 0.0 copy-start.7
  3.0 0.7 copy-done.7
  3.7 0.0 copy-start.1
  3.7 30.5 %flows.1 = (f32[16,32,128]{2,1,0:T(8,128)S(1)}, f32[8,32,128]{2,1,0:T(8,128)S(1)}) custom-call(bf16[32,512]{1,0:T(8,128)(2,1)S(1)} %copy-done.6, bf16[2048,512]{1,0:T(8,128)(2,1)S(1)} %copy-done, s32[1,1024]{1,0:T(1,128)S(1)} %bitcast.2), custom_call_target="tpu_custom_call" | custom-call | tf_op jit(solution)/shard_map/flows/pallas_call | solution.py:141
  34.2 0.0 copy-start.2
  34.2 0.7 copy-done.2
  34.9 0.0 copy-start.4
  35.0 0.6 copy-done.4
  35.6 29.6 %terms.1 = (f32[16,32,128]{2,1,0:T(8,128)}, f32[8,32,128]{2,1,0:T(8,128)}) custom-call(s32[1,16]{1,0:T(1,128)} %list_ref.1, s32[1]{0:T(128)S(6)} %copy.9.count_ref, bf16[1024,2048]{1,0:T(8,128)(2,1)} %of_ref.1, f32[16,32,128]{2,1,0:T(8,128)} %copy-done.2, f32[1,2048]{1,0:T(1,128)} %bitcast.4, f32[8,32,128]{2,1,0:T(8,128)} %copy-done.4), custom_call_target="tpu_custom_call" | custom-call | tf_op jit(solution)/shard_map/terms/pallas_call | solution.py:249
  65.2 0.0 copy-done.8
  65.2 0.0 copy-done.1
  65.2 0.0 copy-start.3
  65.2 0.9 copy-done.3
  66.2 0.0 copy-start.5
  66.2 0.9 copy-done.5
  67.1 71.1 %grads.1 = f32[32,512]{1,0:T(8,128)S(1)} custom-call(f32[16,32,128]{2,1,0:T(8,128)S(1)} %copy-done.3, f32[8,32,128]{2,1,0:T(8,128)S(1)} %copy-done.5, s32[1,1024]{1,0:T(1,128)S(1)} %bitcast.3, bf16[2048,512]{1,0:T(8,128)(2,1)S(1)} %copy-done.1), custom_call_target="tpu_custom_call" | custom-call | tf_op jit(solution)/shard_map/grads/pallas_call | solution.py:328
  138.2 0.6 copy.10
Async XLA Ops:
  0.0 65.2 %copy-start.8 = (s32[1024]{0:T(1024)S(1)}, s32[1024]{0:T(1024)}, u32[]{:S(2)}) copy-start(s32[1024]{0:T(1024)} %param.11) | copy-start | bytes 12292
  0.7 1.6 %copy-start = (bf16[2048,512]{1,0:T(8,128)(2,1)S(1)}, bf16[2048,512]{1,0:T(8,128)(2,1)}, u32[]{:S(2)}) copy-start(bf16[2048,512]{1,0:T(8,128)(2,1)} %sf_ref.3) | copy-start | bytes 6291460
  2.3 0.8 copy-start.6
  3.0 0.7 copy-start.7
  3.7 61.5 %copy-start.1 = (bf16[2048,512]{1,0:T(8,128)(2,1)S(1)}, bf16[2048,512]{1,0:T(8,128)(2,1)}, u32[]{:S(2)}) copy-start(bf16[2048,512]{1,0:T(8,128)(2,1)} %sf_ref.3) | copy-start | bytes 6291460
  34.2 0.7 copy-start.2
  34.9 0.6 copy-start.4
  65.2 1.0 copy-start.3
  66.2 0.9 copy-start.5

commit v3 on v2

v3 whole, which is shorter than its diff:
```python
import functools

import jax
import jax.numpy as jnp
from jax import lax
from jax.experimental import pallas as pl
from jax.experimental.pallas import tpu as pltpu
from jax.sharding import PartitionSpec as P

CASES = 32
NO = 16384
TILE = 64
GROUP = 4
LB = 128
F32 = jnp.float32
BF16 = jnp.bfloat16
MESH = pl.DeviceIdType.MESH
VMEM = pl.BlockSpec(memory_space=pltpu.VMEM)
SMEM = pl.BlockSpec(memory_space=pltpu.SMEM)
HBM = pl.BlockSpec(memory_space=pltpu.HBM)


LINE_STEPS = [(1, 2), (1, 1), (1, 3), (0, 2), (1, 0), (0, 1), (0, 3)]
OUT_STEPS = [(x, y, c) for x, y in [(1, 2), (1, 1), (1, 3), (0, 2), (1, 0), (0, 1), (0, 3)] for c in (1, 0)]
OUT_STEPS += [(0, 0, 1)]
STEPS = {"line": LINE_STEPS, "out": OUT_STEPS}


def partner(axis, i):
    me = lax.axis_index(axis)
    if axis == "line":
        dx, dz = LINE_STEPS[i]
        return lax.rem(me // 4 + dx, 2) * 4 + lax.rem(lax.rem(me, 4) + dz, 4)
    dx, dy, dc = OUT_STEPS[i]
    x, y, c = me // 8, lax.rem(me // 2, 4), lax.rem(me, 2)
    return lax.rem(x + dx, 2) * 8 + lax.rem(y + dy, 4) * 2 + lax.rem(c + dc, 2)


def peer(axis, i):
    if axis == "out":
        return (lax.axis_index("line"), partner(axis, i))
    return (partner(axis, i), lax.axis_index("out"))


def greet():
    barrier = pltpu.get_barrier_semaphore()
    for axis in ("out", "line"):
        for i in range(len(STEPS[axis])):
            pl.semaphore_signal(barrier, inc=1, device_id=peer(axis, i), device_id_type=MESH)
    return barrier


def send(src, dst, sems, i, axis):
    copy = pltpu.make_async_remote_copy(
        src_ref=src,
        dst_ref=dst,
        send_sem=sems.at[0, i],
        recv_sem=sems.at[1, i],
        device_id=peer(axis, i),
        device_id_type=MESH,
    )
    copy.start()
    return copy


def split3(x):
    hi = x.astype(BF16)
    rest = x - hi.astype(F32)
    mid = rest.astype(BF16)
    low = (rest - mid.astype(F32)).astype(BF16)
    return jnp.concatenate([hi, mid, low], axis=0)


def send_parts(parts, recv, sems, axis, fill=None):
    copies = []
    for i in range(len(STEPS[axis])):
        d = partner(axis, i)
        if fill is not None:
            fill(d)
        copies.append(send(parts.at[d], recv.at[i], sems, i, axis))
    if fill is not None:
        fill(lax.axis_index(axis))
    return copies


def sum_parts(parts, recv, copies, axis):
    total = parts[lax.axis_index(axis)]
    for i in reversed(range(len(copies))):
        copies[i].wait_recv()
        total = total + recv[i]
    return total


def finish(copies):
    for copy in copies:
        copy.wait_send()


def spread(slots, sems, axis):
    me = lax.axis_index(axis)
    copies = [send(slots.at[me], slots.at[me], sems, i, axis) for i in range(len(STEPS[axis]))]
    for copy in copies:
        copy.wait_recv()
    return copies


def hot_table(hot, line_ref, n_out, n_k):
    local = line_ref[...] - lax.axis_index("line") * (n_out * LB)

    def hot_rows(r, _):
        base = pl.multiple_of(r * LB, LB)
        ids = lax.broadcasted_iota(jnp.int32, (LB, n_k), 0) + base
        hot[pl.ds(base, LB), :] = (ids == local).astype(F32).astype(BF16)
        return 0

    lax.fori_loop(0, n_out, hot_rows, 0)


def flows_kernel(
    n_line, n_out, inj_ref, sf_ref, line_ref, lf_ref, ff_ref,
    inj, sf, line, parts, recv_o, slots_o, hot, picked, recv_l, slots_l,
    s_in, s_ro, s_go, s_rl, s_gl,
):
    loads = [
        pltpu.make_async_copy(src, dst, s_in.at[i])
        for i, (src, dst) in enumerate([(inj_ref, inj), (sf_ref, sf), (line_ref, line)])
    ]
    for load in loads:
        load.start()
    barrier = greet()
    for load in loads:
        load.wait()
    for d in range(n_out):
        parts[d] = lax.dot_general(
            inj[...], sf[d * LB : (d + 1) * LB, :], (((1,), (1,)), ((), ())), preferred_element_type=F32
        )
    pl.semaphore_wait(barrier, n_out + n_line - 2)
    sent = send_parts(parts, recv_o, s_ro, "out")
    hot_table(hot, line, n_out, n_line * LB)
    slots_o[lax.axis_index("out")] = sum_parts(parts, recv_o, sent, "out")
    sent += spread(slots_o, s_go, "out")
    wide = jnp.concatenate([slots_o[i] for i in range(n_out)], axis=1)
    got = jnp.dot(split3(wide), hot[...], preferred_element_type=F32)
    got = got[:CASES] + got[CASES : 2 * CASES] + got[2 * CASES :]
    for i in range(n_line):
        picked[i] = got[:, i * LB : (i + 1) * LB]
    sent += send_parts(picked, recv_l, s_rl, "line")
    lf_ref[...] = slots_o[...]
    slots_l[lax.axis_index("line")] = sum_parts(picked, recv_l, sent[-len(LINE_STEPS) :], "line")
    sent += spread(slots_l, s_gl, "line")
    ff_ref[...] = slots_l[...]
    finish(sent)


def flows(n_line, n_out, injections, shift_factors, outage_line):
    n_k = n_line * LB
    block = (CASES, LB)
    dma = pltpu.SemaphoreType.DMA
    line_row = outage_line.reshape(1, n_k)
    return pl.pallas_call(
        functools.partial(flows_kernel, n_line, n_out),
        in_specs=[HBM, HBM, HBM],
        out_specs=[VMEM, VMEM],
        out_shape=[
            jax.ShapeDtypeStruct((n_out,) + block, F32),
            jax.ShapeDtypeStruct((n_line,) + block, F32),
        ],
        scratch_shapes=[
            pltpu.VMEM(injections.shape, BF16),
            pltpu.VMEM(shift_factors.shape, BF16),
            pltpu.VMEM(line_row.shape, jnp.int32),
            pltpu.VMEM((n_out,) + block, F32),
            pltpu.VMEM((n_out,) + block, F32),
            pltpu.VMEM((n_out,) + block, F32),
            pltpu.VMEM((n_out * LB, n_k), BF16),
            pltpu.VMEM((n_line,) + block, F32),
            pltpu.VMEM((n_line,) + block, F32),
            pltpu.VMEM((n_line,) + block, F32),
            dma((3,)),
            dma((2, n_out)),
            dma((2, n_out)),
            dma((2, n_line)),
            dma((2, n_line)),
        ],
        compiler_params=pltpu.CompilerParams(
            collective_id=0, has_side_effects=True, vmem_limit_bytes=63 * 2**20
        ),
        name="flows",
    )(injections, shift_factors, line_row)


def terms_kernel(
    n_line, n_out, list_ref, count_ref, of_ref, lf_ref, lim_ref, ff_ref, dir_ref, rev_ref,
    wide_of, low, high, fall, dsum, qsum, turned, rsum,
):
    for t in range(n_out):
        cols = pl.ds(t * LB, LB)
        lim = lim_ref[:, cols]
        flow = lf_ref[t]
        for c in range(CASES):
            low[c, :, cols] = jnp.broadcast_to(-lim - flow[c : c + 1], (8, LB))
            high[c, :, cols] = jnp.broadcast_to(lim - flow[c : c + 1], (8, LB))
    for b in range(n_line):
        turned[b * LB : (b + 1) * LB, 0:CASES] = ff_ref[b].T
    dsum[...] = jnp.zeros_like(dsum)
    qsum[...] = jnp.zeros_like(qsum)
    rsum[...] = jnp.zeros_like(rsum)
    n_sub = TILE // 8
    lanes = lax.broadcasted_iota(jnp.int32, (8, LB), 1)

    def tile_step(step, _):
        tile = list_ref[0, step]
        k0 = pl.multiple_of(tile * TILE, TILE)
        narrow = of_ref[pl.ds(k0, TILE), :]
        wide_of[...] = narrow.astype(F32)
        pair = ff_ref[tile // 2]
        half = lax.rem(tile, 2) == 0
        mine = jnp.where(half, pair[:, :TILE], pair[:, TILE:])
        prod = jnp.dot(split3(mine), narrow, preferred_element_type=F32)
        qsum[...] += prod[:CASES] + prod[CASES : 2 * CASES] + prod[2 * CASES :]
        square = jnp.zeros((TILE, LB), F32)
        for t in range(n_out):
            w = wide_of[:, t * LB : (t + 1) * LB]
            square = square + w * w
        for c in range(CASES):
            fall[c] = jnp.broadcast_to(turned[pl.ds(k0, TILE), c : c + 1], (TILE, LB))

        def reduce_rows(c, sums):
            return tuple(
                jnp.where(lanes == c, jnp.sum(fall[jnp.maximum(c, 0), 8 * i : 8 * i + 8, :], axis=1, keepdims=True), sums[i])
                for i in range(n_sub)
            )

        def case_step(c):
            ffs = [fall[c, 8 * i : 8 * i + 8, :] for i in range(n_sub)]
            acc = [ffs[i] * square[8 * i : 8 * i + 8] for i in range(n_sub)]
            for t in range(n_out):
                cols = pl.ds(t * LB, LB)
                lo = low[c, :, cols]
                hi = high[c, :, cols]
                qs = []
                for i in range(n_sub):
                    o = wide_of[8 * i : 8 * i + 8, t * LB : (t + 1) * LB]
                    q = jnp.minimum(jnp.maximum(ffs[i] * o, lo), hi)
                    acc[i] = acc[i] - q * o
                    qs.append(q)
                while len(qs) > 1:
                    qs = [qs[i] + qs[i + 1] for i in range(0, len(qs), 2)]
                dsum[c, :, cols] += qs[0]
            for i in range(n_sub):
                fall[c, 8 * i : 8 * i + 8, :] = acc[i]

        def group_step(g, sums):
            for e in range(GROUP):
                sums = reduce_rows(g * GROUP - GROUP + e, sums)
            for e in range(GROUP):
                case_step(g * GROUP + e)
            return sums

        zero = jnp.zeros((8, LB), F32)
        sums = lax.fori_loop(0, CASES // GROUP, group_step, (zero,) * n_sub)
        for e in range(GROUP):
            sums = reduce_rows(CASES - GROUP + e, sums)
        for i in range(n_sub):
            rsum[pl.ds(k0 + 8 * i, 8), :] = sums[i]
        return 0

    lax.fori_loop(0, count_ref[0], tile_step, 0)
    for t in range(n_out):
        cols = slice(t * LB, (t + 1) * LB)
        dir_ref[t] = qsum[:, cols] - jnp.sum(dsum[:, :, cols], axis=1)
    for b in range(n_line):
        rev_ref[b] = rsum[b * LB : (b + 1) * LB, :].T[:CASES]


def terms(n_line, n_out, tile_list, tile_count, outage_factors, lf, limits, ff):
    n_l = n_out * LB
    n_k = n_line * LB
    block = (CASES, LB)
    return pl.pallas_call(
        functools.partial(terms_kernel, n_line, n_out),
        in_specs=[SMEM, SMEM, VMEM, VMEM, VMEM, VMEM],
        out_specs=[VMEM, VMEM],
        out_shape=[
            jax.ShapeDtypeStruct((n_out,) + block, F32),
            jax.ShapeDtypeStruct((n_line,) + block, F32),
        ],
        scratch_shapes=[
            pltpu.VMEM((TILE, n_l), F32),
            pltpu.VMEM((CASES, 8, n_l), F32),
            pltpu.VMEM((CASES, 8, n_l), F32),
            pltpu.VMEM((CASES, TILE, LB), F32),
            pltpu.VMEM((CASES, 8, n_l), F32),
            pltpu.VMEM((CASES, n_l), F32),
            pltpu.VMEM((n_k, LB), F32),
            pltpu.VMEM((n_k, LB), F32),
        ],
        compiler_params=pltpu.CompilerParams(vmem_limit_bytes=63 * 2**20),
        name="terms",
    )(tile_list, tile_count, outage_factors, lf, limits.reshape(1, n_l), ff)


def grads_kernel(
    n_line, n_out, dir_ref, rev_ref, line_ref, sf_ref, out_ref,
    line, sf, recv_r, slots_r, hot, parts, recv_o, slots_o, slots_f,
    s_in, s_rr, s_gr, s_ro, s_go, s_gf,
):
    loads = [
        pltpu.make_async_copy(src, dst, s_in.at[i])
        for i, (src, dst) in enumerate([(line_ref, line), (sf_ref, sf)])
    ]
    barrier = greet()
    for load in loads:
        load.start()
    pl.semaphore_wait(barrier, n_out + n_line - 2)
    sent = send_parts(rev_ref, recv_r, s_rr, "line")
    loads[0].wait()
    hot_table(hot, line, n_out, n_line * LB)
    slots_r[lax.axis_index("line")] = sum_parts(rev_ref, recv_r, sent, "line")
    sent += spread(slots_r, s_gr, "line")
    three = split3(jnp.concatenate([slots_r[i] for i in range(n_line)], axis=1))

    def fill(d):
        table = hot[pl.ds(pl.multiple_of(d * LB, LB), LB), :]
        got = lax.dot_general(three, table, (((1,), (1,)), ((), ())), preferred_element_type=F32)
        parts[d] = dir_ref[d] + (got[:CASES] + got[CASES : 2 * CASES] + got[2 * CASES :])

    scattered = send_parts(parts, recv_o, s_ro, "out", fill)
    grad = sum_parts(parts, recv_o, scattered, "out")
    slots_o[lax.axis_index("out")] = (grad * (2.0 / NO)).astype(BF16)
    sent += scattered + spread(slots_o, s_go, "out")
    rounded = jnp.concatenate([slots_o[i] for i in range(n_out)], axis=1)
    loads[1].wait()
    partial = jnp.dot(rounded, sf[...], preferred_element_type=F32)
    slots_f[lax.axis_index("line")] = partial.astype(BF16)
    sent += spread(slots_f, s_gf, "line")
    result = slots_f[0].astype(F32)
    for i in range(1, n_line):
        result = result + slots_f[i].astype(F32)
    out_ref[...] = result
    finish(sent)


def grads(n_line, n_out, direct, reverse, outage_line, shift_factors):
    n_k = n_line * LB
    block = (CASES, LB)
    dma = pltpu.SemaphoreType.DMA
    return pl.pallas_call(
        functools.partial(grads_kernel, n_line, n_out),
        in_specs=[VMEM, VMEM, HBM, HBM],
        out_specs=VMEM,
        out_shape=jax.ShapeDtypeStruct((CASES, shift_factors.shape[1]), F32),
        scratch_shapes=[
            pltpu.VMEM((1, n_k), jnp.int32),
            pltpu.VMEM(shift_factors.shape, BF16),
            pltpu.VMEM((n_line,) + block, F32),
            pltpu.VMEM((n_line,) + block, F32),
            pltpu.VMEM((n_out * LB, n_k), BF16),
            pltpu.VMEM((n_out,) + block, F32),
            pltpu.VMEM((n_out,) + block, F32),
            pltpu.VMEM((n_out,) + block, BF16),
            pltpu.VMEM((n_line, CASES, shift_factors.shape[1]), BF16),
            dma((2,)),
            dma((2, n_line)),
            dma((2, n_line)),
            dma((2, n_out)),
            dma((2, n_out)),
            dma((2, n_line)),
        ],
        compiler_params=pltpu.CompilerParams(
            collective_id=1, has_side_effects=True, vmem_limit_bytes=63 * 2**20
        ),
        name="grads",
    )(direct, reverse, outage_line.reshape(1, n_k), shift_factors)


def shards(
    n_line, n_out, injections, shift_factors, outage_factors, limits, outage_line, tile_list, tile_count
):
    lf, ff = flows(n_line, n_out, injections, shift_factors, outage_line)
    direct, reverse = terms(n_line, n_out, tile_list, tile_count, outage_factors, lf, limits, ff)
    return grads(n_line, n_out, direct, reverse, outage_line, shift_factors)


def solution(mesh):
    placed = (
        P(None, "out"),
        P("line", "out"),
        P("out", "line"),
        P("line"),
        P("out"),
        P("out", None),
        P("out"),
    )
    return jax.shard_map(
        functools.partial(shards, mesh.shape["line"], mesh.shape["out"]),
        mesh=mesh,
        in_specs=placed,
        out_specs=P(None, "out"),
        check_vma=False,
    )
```

time: 139 us -> 134 us (0.964)
  local copies, waits for them, and re-layouts: 6.86 us -> 1.47 us
    pallas_call x1, Pallas kernels: 29.6 us -> 57.6 us  [terms(): pl.pallas_call(functools.partial(terms_kernel, n_line, n_out), in_specs=[...]
    pallas_call x1, Pallas kernels: 71.1 us -> 44 us  [grads(): pl.pallas_call(functools.partial(grads_kernel, n_line, n_out), in_specs=[...]
    unnamed x19 -> x1, local copies, waits for them, and re-layouts: 6.86 us -> 1.47 us
where the time goes in v3:
time: 134 us
  Pallas kernels  132 us (99%)
  local copies, waits for them, and re-layouts  1.47 us (1%)
    pallas_call x1, Pallas kernels, terms(): pl.pallas_call(functools.partial(terms_kernel, n_line, n_out), in_specs=[...  57.6 us
    pallas_call x1, Pallas kernels, grads(): pl.pallas_call(functools.partial(grads_kernel, n_line, n_out), in_specs=[...  44 us
    pallas_call x1, Pallas kernels, flows(): pl.pallas_call(functools.partial(flows_kernel, n_line, n_out), in_specs=[...  29.9 us

profile of v3, /device:TPU:0, one launch (start us, length us, event | category | flops | bytes accessed | tf_op | source)
XLA Modules:
  0.0 133.7 jit_solution(1273547731294577620)
XLA Ops:
  0.7 29.9 %flows.1 = (f32[16,32,128]{2,1,0:T(8,128)}, f32[8,32,128]{2,1,0:T(8,128)}) custom-call(bf16[32,512]{1,0:T(8,128)(2,1)} %inj_ref.1, bf16[2048,512]{1,0:T(8,128)(2,1)} %sf_ref.3, s32[1,1024]{1,0:T(1,128)} %bitcast.2), custom_call_target="tpu_custom_call" | custom-call | tf_op jit(solution)/shard_map/flows/pallas_call | solution.py:160
  30.6 57.6 %terms.1 = (f32[16,32,128]{2,1,0:T(8,128)}, f32[8,32,128]{2,1,0:T(8,128)}) custom-call(s32[1,16]{1,0:T(1,128)} %list_ref.1, s32[1]{0:T(128)S(6)} %copy.9.count_ref, bf16[1024,2048]{1,0:T(8,128)(2,1)} %of_ref.1, f32[16,32,128]{2,1,0:T(8,128)} %get-tuple-element.9.lf_ref, f32[1,2048]{1,0:T(1,128)} %bitcast.4, f32[8,32,128]{2,1,0:T(8,128)} %get-tuple-element.10.ff_ref), custom_call_target="tpu_custom_call" | custom-call | tf_op jit(solution)/shard_map/terms/pallas_call | solution.py:280
  88.2 44.0 %grads.1 = f32[32,512]{1,0:T(8,128)} custom-call(f32[16,32,128]{2,1,0:T(8,128)} %get-tuple-element.11.dir_ref, f32[8,32,128]{2,1,0:T(8,128)} %get-tuple-element.12.rev_ref, s32[1,1024]{1,0:T(1,128)} %bitcast.3, bf16[2048,512]{1,0:T(8,128)(2,1)} %sf_ref.3), custom_call_target="tpu_custom_call" | custom-call | tf_op jit(solution)/shard_map/grads/pallas_call | solution.py:348
  132.2 1.5 %copy.10 = f32[32,512]{1,0:T(8,128)} copy(f32[32,512]{1,0:T(8,128)} %grads.1) | data formatting | bytes 131072

commit v4 on v3

v4 whole, which is shorter than its diff:
```python
import functools

import jax
import jax.numpy as jnp
from jax import lax
from jax.experimental import pallas as pl
from jax.experimental.pallas import tpu as pltpu
from jax.sharding import PartitionSpec as P

CASES = 32
NO = 16384
TILE = 64
GROUP = 4
LB = 128
F32 = jnp.float32
BF16 = jnp.bfloat16
MESH = pl.DeviceIdType.MESH
VMEM = pl.BlockSpec(memory_space=pltpu.VMEM)
HBM = pl.BlockSpec(memory_space=pltpu.HBM)


LINE_STEPS = [(1, 2), (1, 1), (1, 3), (0, 2), (1, 0), (0, 1), (0, 3)]
OUT_STEPS = [(x, y, c) for x, y in [(1, 2), (1, 1), (1, 3), (0, 2), (1, 0), (0, 1), (0, 3)] for c in (1, 0)]
OUT_STEPS += [(0, 0, 1)]
STEPS = {"line": LINE_STEPS, "out": OUT_STEPS}


def partner(axis, i):
    me = lax.axis_index(axis)
    if axis == "line":
        dx, dz = LINE_STEPS[i]
        return lax.rem(me // 4 + dx, 2) * 4 + lax.rem(lax.rem(me, 4) + dz, 4)
    dx, dy, dc = OUT_STEPS[i]
    x, y, c = me // 8, lax.rem(me // 2, 4), lax.rem(me, 2)
    return lax.rem(x + dx, 2) * 8 + lax.rem(y + dy, 4) * 2 + lax.rem(c + dc, 2)


def peer(axis, i):
    if axis == "out":
        return (lax.axis_index("line"), partner(axis, i))
    return (partner(axis, i), lax.axis_index("out"))


def greet():
    barrier = pltpu.get_barrier_semaphore()
    for axis in ("out", "line"):
        for i in range(len(STEPS[axis])):
            pl.semaphore_signal(barrier, inc=1, device_id=peer(axis, i), device_id_type=MESH)
    return barrier


def send(src, dst, sems, i, axis):
    copy = pltpu.make_async_remote_copy(
        src_ref=src,
        dst_ref=dst,
        send_sem=sems.at[0, i],
        recv_sem=sems.at[1, i],
        device_id=peer(axis, i),
        device_id_type=MESH,
    )
    copy.start()
    return copy


def split3(x):
    hi = x.astype(BF16)
    rest = x - hi.astype(F32)
    mid = rest.astype(BF16)
    low = (rest - mid.astype(F32)).astype(BF16)
    return jnp.concatenate([hi, mid, low], axis=0)


def send_parts(parts, recv, sems, axis, fill=None):
    copies = []
    for i in range(len(STEPS[axis])):
        d = partner(axis, i)
        if fill is not None:
            fill(d)
        copies.append(send(parts.at[d], recv.at[i], sems, i, axis))
    if fill is not None:
        fill(lax.axis_index(axis))
    return copies


def sum_parts(parts, recv, copies, axis):
    total = parts[lax.axis_index(axis)]
    for i in reversed(range(len(copies))):
        copies[i].wait_recv()
        total = total + recv[i]
    return total


def finish(copies):
    for copy in copies:
        copy.wait_send()


def spread(slots, sems, axis, meanwhile=None):
    me = lax.axis_index(axis)
    copies = [send(slots.at[me], slots.at[me], sems, i, axis) for i in range(len(STEPS[axis]))]
    if meanwhile is not None:
        meanwhile()
    for copy in copies:
        copy.wait_recv()
    return copies


def hot_table(hot, line_ref, n_out, n_k):
    local = line_ref[...] - lax.axis_index("line") * (n_out * LB)

    def hot_rows(r, _):
        base = pl.multiple_of(r * LB, LB)
        ids = lax.broadcasted_iota(jnp.int32, (LB, n_k), 0) + base
        hot[pl.ds(base, LB), :] = (ids == local).astype(F32).astype(BF16)
        return 0

    lax.fori_loop(0, n_out, hot_rows, 0)


def add3(x):
    return x[:CASES] + x[CASES : 2 * CASES] + x[2 * CASES :]


def gradient_kernel(
    n_line, n_out, inj_hbm, sf_hbm, of_hbm, lim_hbm, line_hbm, list_ref, count_ref, out_ref,
    inj, sf, of, lim, line, parts, recv_o, slots_o, hot, picked, recv_l, slots_l,
    wide_of, square, low, high, fall, dsum, qsum, turned, rsum, act,
    rev, recv_r, slots_r, terms, recv_t, slots_g, slots_f,
    s_in, s_ro, s_go, s_rl, s_gl, s_rr, s_gr, s_rt, s_gg, s_gf,
):
    n_k = n_line * LB
    n_tiles = n_k // TILE
    n_sub = TILE // 8
    me_line = lax.axis_index("line")
    me_out = lax.axis_index("out")
    loads = [
        pltpu.make_async_copy(src, dst, s_in.at[i])
        for i, (src, dst) in enumerate(
            [(inj_hbm, inj), (sf_hbm, sf), (line_hbm, line), (lim_hbm, lim), (of_hbm, of)]
        )
    ]
    for load in loads:
        load.start()
    barrier = greet()

    def widen(first, last):
        def one(tile, _):
            rows = pl.ds(pl.multiple_of(tile * TILE, TILE), TILE)
            total = jnp.zeros((TILE, LB), F32)
            for t in range(n_out):
                w = of[rows, t * LB : (t + 1) * LB].astype(F32)
                wide_of[rows, t * LB : (t + 1) * LB] = w
                total = total + w * w
            square[rows, :] = total
            return 0

        lax.fori_loop(first, last, one, 0)

    loads[0].wait()
    loads[1].wait()
    for d in range(n_out):
        parts[d] = lax.dot_general(
            inj[...], sf[d * LB : (d + 1) * LB, :], (((1,), (1,)), ((), ())), preferred_element_type=F32
        )
    pl.semaphore_wait(barrier, n_out + n_line - 2)
    sent = send_parts(parts, recv_o, s_ro, "out")
    for load in loads[2:]:
        load.wait()
    hot_table(hot, line, n_out, n_k)
    widen(0, n_tiles // 2)
    slots_o[me_out] = sum_parts(parts, recv_o, sent, "out")
    sent += spread(slots_o, s_go, "out", lambda: widen(n_tiles // 2, n_tiles))
    flow = jnp.concatenate([slots_o[i] for i in range(n_out)], axis=1)
    got = add3(jnp.dot(split3(flow), hot[...], preferred_element_type=F32))
    for i in range(n_line):
        picked[i] = got[:, i * LB : (i + 1) * LB]
    picks = send_parts(picked, recv_l, s_rl, "line")
    sent += picks
    for t in range(n_out):
        cols = slice(t * LB, (t + 1) * LB)
        for c in range(CASES):
            low[c, :, cols] = jnp.broadcast_to(-lim[:, cols] - slots_o[t, c : c + 1, :], (8, LB))
            high[c, :, cols] = jnp.broadcast_to(lim[:, cols] - slots_o[t, c : c + 1, :], (8, LB))
    slots_l[me_line] = sum_parts(picked, recv_l, picks, "line")

    def clear():
        dsum[...] = jnp.zeros_like(dsum)
        qsum[...] = jnp.zeros_like(qsum)
        ids = lax.broadcasted_iota(jnp.int32, (n_tiles, n_tiles), 0)
        place = lax.broadcasted_iota(jnp.int32, (n_tiles, n_tiles), 1)
        listed = (list_ref[...] == ids) & (place < count_ref[...])
        flags = jnp.sum(jnp.where(listed, 1.0, 0.0), axis=1, keepdims=True)
        act[...] = jnp.broadcast_to(flags, (n_tiles, LB))

    sent += spread(slots_l, s_gl, "line", clear)
    for b in range(n_line):
        turned[b * LB : (b + 1) * LB, 0:CASES] = slots_l[b].T
    lanes = lax.broadcasted_iota(jnp.int32, (TILE, LB), 1)

    def tile_step(tile, _):
        k0 = pl.multiple_of(tile * TILE, TILE)
        rows = pl.ds(k0, TILE)
        on = act[pl.ds(tile, 1), :]
        pair = slots_l[tile // 2]
        mine = jnp.where(lax.rem(tile, 2) == 0, pair[:, :TILE], pair[:, TILE:]) * on[:, :TILE]
        qsum[...] += add3(jnp.dot(split3(mine), of[rows, :], preferred_element_type=F32))
        for c in range(CASES):
            fall[c] = jnp.broadcast_to(turned[rows, c : c + 1], (TILE, LB))

        def reduce_rows(c, sums):
            return jnp.where(lanes == c, jnp.sum(fall[jnp.maximum(c, 0)], axis=1, keepdims=True), sums)

        def case_step(c):
            ffs = fall[c]
            acc = ffs * square[rows, :]
            for t in range(n_out):
                cols = slice(t * LB, (t + 1) * LB)
                lo = jnp.concatenate([low[c, :, cols]] * n_sub, axis=0)
                hi = jnp.concatenate([high[c, :, cols]] * n_sub, axis=0)
                o = wide_of[rows, cols]
                q = jnp.minimum(jnp.maximum(ffs * o, lo), hi)
                acc = acc - q * o
                size = TILE // 2
                while size >= 8:
                    q = q[:size] + q[size:]
                    size //= 2
                dsum[c, :, cols] += q * on
            fall[c] = acc

        def group_step(g, sums):
            for e in range(GROUP):
                sums = reduce_rows(g * GROUP - GROUP + e, sums)
            for e in range(GROUP):
                case_step(g * GROUP + e)
            return sums

        sums = lax.fori_loop(0, CASES // GROUP, group_step, jnp.zeros((TILE, LB), F32))
        for e in range(GROUP):
            sums = reduce_rows(CASES - GROUP + e, sums)
        rsum[rows, :] = sums * on
        return 0

    lax.fori_loop(0, n_tiles, tile_step, 0)

    for b in range(n_line):
        rev[b] = rsum[b * LB : (b + 1) * LB, :].T[:CASES]
    turns = send_parts(rev, recv_r, s_rr, "line")
    sent += turns
    for t in range(n_out):
        cols = slice(t * LB, (t + 1) * LB)
        terms[t] = qsum[:, cols] - jnp.sum(dsum[:, :, cols], axis=1)
    slots_r[me_line] = sum_parts(rev, recv_r, turns, "line")
    sent += spread(slots_r, s_gr, "line")
    three = split3(jnp.concatenate([slots_r[i] for i in range(n_line)], axis=1))

    def fill(d):
        table = hot[pl.ds(pl.multiple_of(d * LB, LB), LB), :]
        terms[d] += add3(
            lax.dot_general(three, table, (((1,), (1,)), ((), ())), preferred_element_type=F32)
        )

    scattered = send_parts(terms, recv_t, s_rt, "out", fill)
    grad = sum_parts(terms, recv_t, scattered, "out")
    slots_g[me_out] = (grad * (2.0 / NO)).astype(BF16)
    sent += scattered + spread(slots_g, s_gg, "out")
    rounded = jnp.concatenate([slots_g[i] for i in range(n_out)], axis=1)
    partial = jnp.dot(rounded, sf[...], preferred_element_type=F32)
    slots_f[me_line] = partial.astype(BF16)
    sent += spread(slots_f, s_gf, "line")
    result = slots_f[0].astype(F32)
    for i in range(1, n_line):
        result = result + slots_f[i].astype(F32)
    out_ref[...] = result
    finish(sent)


def shards(
    n_line, n_out, injections, shift_factors, outage_factors, limits, outage_line, tile_list, tile_count
):
    n_k = n_line * LB
    n_l = n_out * LB
    block = (CASES, LB)
    dma = pltpu.SemaphoreType.DMA
    line_row = outage_line.reshape(1, n_k)
    limit_row = limits.reshape(1, n_l)
    per_line = pltpu.VMEM((n_line,) + block, F32)
    per_out = pltpu.VMEM((n_out,) + block, F32)
    return pl.pallas_call(
        functools.partial(gradient_kernel, n_line, n_out),
        in_specs=[HBM] * 5 + [VMEM] * 2,
        out_specs=VMEM,
        out_shape=jax.ShapeDtypeStruct((CASES, shift_factors.shape[1]), F32),
        scratch_shapes=[
            pltpu.VMEM(injections.shape, BF16),
            pltpu.VMEM(shift_factors.shape, BF16),
            pltpu.VMEM(outage_factors.shape, BF16),
            pltpu.VMEM(limit_row.shape, F32),
            pltpu.VMEM(line_row.shape, jnp.int32),
            per_out,
            per_out,
            per_out,
            pltpu.VMEM((n_l, n_k), BF16),
            per_line,
            per_line,
            per_line,
            pltpu.VMEM((n_k, n_l), F32),
            pltpu.VMEM((n_k, LB), F32),
            pltpu.VMEM((CASES, 8, n_l), F32),
            pltpu.VMEM((CASES, 8, n_l), F32),
            pltpu.VMEM((CASES, TILE, LB), F32),
            pltpu.VMEM((CASES, 8, n_l), F32),
            pltpu.VMEM((CASES, n_l), F32),
            pltpu.VMEM((n_k, LB), F32),
            pltpu.VMEM((n_k, LB), F32),
            pltpu.VMEM((n_k // TILE, LB), F32),
            per_line,
            per_line,
            per_line,
            per_out,
            per_out,
            pltpu.VMEM((n_out,) + block, BF16),
            pltpu.VMEM((n_line, CASES, shift_factors.shape[1]), BF16),
            dma((5,)),
            dma((2, n_out)),
            dma((2, n_out)),
            dma((2, n_line)),
            dma((2, n_line)),
            dma((2, n_line)),
            dma((2, n_line)),
            dma((2, n_out)),
            dma((2, n_out)),
            dma((2, n_line)),
        ],
        compiler_params=pltpu.CompilerParams(
            collective_id=0, has_side_effects=True, vmem_limit_bytes=63 * 2**20
        ),
        name="gradient",
    )(injections, shift_factors, outage_factors, limit_row, line_row, tile_list, tile_count.reshape(1, 1))


def solution(mesh):
    placed = (
        P(None, "out"),
        P("line", "out"),
        P("out", "line"),
        P("line"),
        P("out"),
        P("out", None),
        P("out"),
    )
    return jax.shard_map(
        functools.partial(shards, mesh.shape["line"], mesh.shape["out"]),
        mesh=mesh,
        in_specs=placed,
        out_specs=P(None, "out"),
        check_vma=False,
    )
```

time: 134 us -> 128 us (0.955)
  Pallas kernels: 132 us -> 126 us
    pallas_call x3 -> x1, Pallas kernels: 132 us -> 126 us  [shards(): pl.pallas_call(functools.partial(gradient_kernel, n_line, n_out), in_spec...]
where the time goes in v4:
time: 128 us
  Pallas kernels  126 us (98%)
  local copies, waits for them, and re-layouts  1.47 us (1%)
    pallas_call x1, Pallas kernels, shards(): pl.pallas_call(functools.partial(gradient_kernel, n_line, n_out), in_spec...  126 us

profile of v4, /device:TPU:0, one launch (start us, length us, event | category | flops | bytes accessed | tf_op | source)
XLA Modules:
  0.0 127.8 jit_solution(14075345386496392888)
XLA Ops:
  0.7 125.6 %gradient.1 = f32[32,512]{1,0:T(8,128)} custom-call(bf16[32,512]{1,0:T(8,128)(2,1)} %inj_hbm.1, bf16[2048,512]{1,0:T(8,128)(2,1)} %sf_hbm.1, bf16[1024,2048]{1,0:T(8,128)(2,1)} %of_hbm.1, f32[1,2048]{1,0:T(1,128)} %bitcast.4, s32[1,1024]{1,0:T(1,128)} %bitcast.5, s32[1,16]{1,0:T(1,128)} %list_ref.1, s32[1,1]{1,0:T(1,128)} %bitcast.3.count_ref), custom_call_target="tpu_custom_call" | custom-call | tf_op jit(solution)/shard_map/gradient/pallas_call | solution.py:288
  126.3 1.5 %copy.10 = f32[32,512]{1,0:T(8,128)} copy(f32[32,512]{1,0:T(8,128)} %gradient.1) | data formatting | bytes 131072

commit v5 on v4

--- a/solution.py
+++ b/solution.py
@@ -22,6 +22,8 @@
 LINE_STEPS = [(1, 2), (1, 1), (1, 3), (0, 2), (1, 0), (0, 1), (0, 3)]
 OUT_STEPS = [(x, y, c) for x, y in [(1, 2), (1, 1), (1, 3), (0, 2), (1, 0), (0, 1), (0, 3)] for c in (1, 0)]
 OUT_STEPS += [(0, 0, 1)]
+FALL_PIECES = [(0, 1), (1, 1), (2, 6)]
+TERM_PIECES = [(0, 4), (4, 3), (7, 1)]
 STEPS = {"line": LINE_STEPS, "out": OUT_STEPS}
 
 
@@ -117,6 +119,17 @@
     lax.fori_loop(0, n_out, hot_rows, 0)
 
 
+def message(src, dst, sems, m, i, piece):
+    return pltpu.make_async_remote_copy(
+        src_ref=src.at[pl.ds(*piece)],
+        dst_ref=dst.at[i, pl.ds(*piece)],
+        send_sem=sems.at[0, m, i],
+        recv_sem=sems.at[1, m, i],
+        device_id=peer("line", i),
+        device_id_type=MESH,
+    )
+
+
 def add3(x):
     return x[:CASES] + x[CASES : 2 * CASES] + x[2 * CASES :]
 
@@ -125,8 +138,8 @@
     n_line, n_out, inj_hbm, sf_hbm, of_hbm, lim_hbm, line_hbm, list_ref, count_ref, out_ref,
     inj, sf, of, lim, line, parts, recv_o, slots_o, hot, picked, recv_l, slots_l,
     wide_of, square, low, high, fall, dsum, qsum, turned, rsum, act,
-    rev, recv_r, slots_r, terms, recv_t, slots_g, slots_f,
-    s_in, s_ro, s_go, s_rl, s_gl, s_rr, s_gr, s_rt, s_gg, s_gf,
+    rev, recv_r, terms, recv_t, slots_g, slots_f,
+    s_in, s_ro, s_go, s_rl, s_rr, s_rt, s_gg, s_gf,
 ):
     n_k = n_line * LB
     n_tiles = n_k // TILE
@@ -174,27 +187,34 @@
     got = add3(jnp.dot(split3(flow), hot[...], preferred_element_type=F32))
     for i in range(n_line):
         picked[i] = got[:, i * LB : (i + 1) * LB]
-    picks = send_parts(picked, recv_l, s_rl, "line")
-    sent += picks
+    falls = [[message(picked, recv_l, s_rl, m, i, FALL_PIECES[m]) for i in range(n_line - 1)] for m in range(3)]
+    for piece in falls:
+        for copy in piece:
+            copy.start()
     for t in range(n_out):
         cols = slice(t * LB, (t + 1) * LB)
         for c in range(CASES):
             low[c, :, cols] = jnp.broadcast_to(-lim[:, cols] - slots_o[t, c : c + 1, :], (8, LB))
             high[c, :, cols] = jnp.broadcast_to(lim[:, cols] - slots_o[t, c : c + 1, :], (8, LB))
-    slots_l[me_line] = sum_parts(picked, recv_l, picks, "line")
-
-    def clear():
-        dsum[...] = jnp.zeros_like(dsum)
-        qsum[...] = jnp.zeros_like(qsum)
-        ids = lax.broadcasted_iota(jnp.int32, (n_tiles, n_tiles), 0)
-        place = lax.broadcasted_iota(jnp.int32, (n_tiles, n_tiles), 1)
-        listed = (list_ref[...] == ids) & (place < count_ref[...])
-        flags = jnp.sum(jnp.where(listed, 1.0, 0.0), axis=1, keepdims=True)
-        act[...] = jnp.broadcast_to(flags, (n_tiles, LB))
-
-    sent += spread(slots_l, s_gl, "line", clear)
-    for b in range(n_line):
-        turned[b * LB : (b + 1) * LB, 0:CASES] = slots_l[b].T
+    dsum[...] = jnp.zeros_like(dsum)
+    qsum[...] = jnp.zeros_like(qsum)
+    ids = lax.broadcasted_iota(jnp.int32, (n_tiles, n_tiles), 0)
+    place = lax.broadcasted_iota(jnp.int32, (n_tiles, n_tiles), 1)
+    listed = (list_ref[...] == ids) & (place < count_ref[...])
+    flags = jnp.sum(jnp.where(listed, 1.0, 0.0), axis=1, keepdims=True)
+    act[...] = jnp.broadcast_to(flags, (n_tiles, LB))
+
+    def take_falls(m):
+        first, many = FALL_PIECES[m]
+        for i in range(n_line - 1):
+            falls[m][i].wait_recv()
+        for b in range(first, first + many):
+            total = picked[b]
+            for i in range(n_line - 1):
+                total = total + recv_l[i, b]
+            slots_l[b] = total
+            turned[b * LB : (b + 1) * LB, 0:CASES] = total.T
+
     lanes = lax.broadcasted_iota(jnp.int32, (TILE, LB), 1)
 
     def tile_step(tile, _):
@@ -204,8 +224,9 @@
         pair = slots_l[tile // 2]
         mine = jnp.where(lax.rem(tile, 2) == 0, pair[:, :TILE], pair[:, TILE:]) * on[:, :TILE]
         qsum[...] += add3(jnp.dot(split3(mine), of[rows, :], preferred_element_type=F32))
+        masked = turned[rows, :] * on
         for c in range(CASES):
-            fall[c] = jnp.broadcast_to(turned[rows, c : c + 1], (TILE, LB))
+            fall[c] = jnp.broadcast_to(masked[:, c : c + 1], (TILE, LB))
 
         def reduce_rows(c, sums):
             return jnp.where(lanes == c, jnp.sum(fall[jnp.maximum(c, 0)], axis=1, keepdims=True), sums)
@@ -224,7 +245,7 @@
                 while size >= 8:
                     q = q[:size] + q[size:]
                     size //= 2
-                dsum[c, :, cols] += q * on
+                dsum[c, :, cols] += q
             fall[c] = acc
 
         def group_step(g, sums):
@@ -240,24 +261,57 @@
         rsum[rows, :] = sums * on
         return 0
 
-    lax.fori_loop(0, n_tiles, tile_step, 0)
-
-    for b in range(n_line):
-        rev[b] = rsum[b * LB : (b + 1) * LB, :].T[:CASES]
-    turns = send_parts(rev, recv_r, s_rr, "line")
-    sent += turns
+    turns = [[message(rev, recv_r, s_rr, m, i, TERM_PIECES[m]) for i in range(n_line - 1)] for m in range(3)]
+
+    def block_step(b, _):
+        for m in range(3):
+
+            @pl.when(b == FALL_PIECES[m][0])
+            def _():
+                take_falls(m)
+
+        lax.fori_loop(b * (LB // TILE), (b + 1) * (LB // TILE), tile_step, 0)
+        rev[b] = rsum[pl.ds(pl.multiple_of(b * LB, LB), LB), :].T[:CASES]
+        for m in range(3):
+
+            @pl.when(b == sum(TERM_PIECES[m]) - 1)
+            def _():
+                for copy in turns[m]:
+                    copy.start()
+
+        return 0
+
+    lax.fori_loop(0, n_line, block_step, 0)
+
+    idle = TILE * (n_tiles - jnp.sum(act[...], axis=0, keepdims=True))
     for t in range(n_out):
         cols = slice(t * LB, (t + 1) * LB)
-        terms[t] = qsum[:, cols] - jnp.sum(dsum[:, :, cols], axis=1)
-    slots_r[me_line] = sum_parts(rev, recv_r, turns, "line")
-    sent += spread(slots_r, s_gr, "line")
-    three = split3(jnp.concatenate([slots_r[i] for i in range(n_line)], axis=1))
+        rest = jnp.minimum(jnp.maximum(0.0, low[:, 0, cols]), high[:, 0, cols])
+        terms[t] = qsum[:, cols] - (jnp.sum(dsum[:, :, cols], axis=1) - idle * rest)
+
+    def summed(m):
+        first, many = TERM_PIECES[m]
+        for i in range(n_line - 1):
+            turns[m][i].wait_recv()
+        blocks = []
+        for b in range(first, first + many):
+            total = rev[b]
+            for i in range(n_line - 1):
+                total = total + recv_r[i, b]
+            blocks.append(total)
+        return blocks
+
+    def placed(three, d, cols):
+        table = hot[pl.ds(pl.multiple_of(d * LB, LB), LB), cols]
+        return add3(lax.dot_general(three, table, (((1,), (1,)), ((), ())), preferred_element_type=F32))
+
+    early = split3(jnp.concatenate(summed(0) + summed(1), axis=1))
+    for t in range(n_out):
+        terms[t] += placed(early, t, slice(0, n_k - LB))
+    late = split3(summed(2)[0])
 
     def fill(d):
-        table = hot[pl.ds(pl.multiple_of(d * LB, LB), LB), :]
-        terms[d] += add3(
-            lax.dot_general(three, table, (((1,), (1,)), ((), ())), preferred_element_type=F32)
-        )
+        terms[d] += placed(late, d, slice(n_k - LB, n_k))
 
     scattered = send_parts(terms, recv_t, s_rt, "out", fill)
     grad = sum_parts(terms, recv_t, scattered, "out")
@@ -271,6 +325,8 @@
     for i in range(1, n_line):
         result = result + slots_f[i].astype(F32)
     out_ref[...] = result
+    for piece in falls + turns:
+        finish(piece)
     finish(sent)
 
 
@@ -301,7 +357,7 @@
             per_out,
             pltpu.VMEM((n_l, n_k), BF16),
             per_line,
-            per_line,
+            pltpu.VMEM((n_line - 1, n_line) + block, F32),
             per_line,
             pltpu.VMEM((n_k, n_l), F32),
             pltpu.VMEM((n_k, LB), F32),
@@ -314,8 +370,7 @@
             pltpu.VMEM((n_k, LB), F32),
             pltpu.VMEM((n_k // TILE, LB), F32),
             per_line,
-            per_line,
-            per_line,
+            pltpu.VMEM((n_line - 1, n_line) + block, F32),
             per_out,
             per_out,
             pltpu.VMEM((n_out,) + block, BF16),
@@ -323,10 +378,8 @@
             dma((5,)),
             dma((2, n_out)),
             dma((2, n_out)),
-            dma((2, n_line)),
-            dma((2, n_line)),
-            dma((2, n_line)),
-            dma((2, n_line)),
+            dma((2, 3, n_line)),
+            dma((2, 3, n_line)),
             dma((2, n_out)),
             dma((2, n_out)),
             dma((2, n_line)),

time: 128 us -> 123 us (0.961)
  Pallas kernels: 126 us -> 119 us
    pallas_call x1, Pallas kernels: 126 us -> 119 us  [shards(): pl.pallas_call(functools.partial(gradient_kernel, n_line, n_out), in_spec...]
where the time goes in v5:
time: 123 us; the launch traced here: 122 us
  Pallas kernels  119 us (97%)
  local copies, waits for them, and re-layouts  1.47 us (1%)
    pallas_call x1, Pallas kernels, shards(): pl.pallas_call(functools.partial(gradient_kernel, n_line, n_out), in_spec...  119 us

profile of v5, /device:TPU:0, one launch (start us, length us, event | category | flops | bytes accessed | tf_op | source)
XLA Modules:
  0.0 121.6 jit_solution(1273305992464758582)
XLA Ops:
  0.7 119.4 %gradient.1 = f32[32,512]{1,0:T(8,128)} custom-call(bf16[32,512]{1,0:T(8,128)(2,1)} %inj_hbm.1, bf16[2048,512]{1,0:T(8,128)(2,1)} %sf_hbm.1, bf16[1024,2048]{1,0:T(8,128)(2,1)} %of_hbm.1, f32[1,2048]{1,0:T(1,128)} %bitcast.4, s32[1,1024]{1,0:T(1,128)} %bitcast.5, s32[1,16]{1,0:T(1,128)} %list_ref.1, s32[1,1]{1,0:T(1,128)} %bitcast.3.count_ref), custom_call_target="tpu_custom_call" | custom-call | tf_op jit(solution)/shard_map/gradient/pallas_call | solution.py:344
  120.1 1.5 %copy.10 = f32[32,512]{1,0:T(8,128)} copy(f32[32,512]{1,0:T(8,128)} %gradient.1) | data formatting | bytes 131072

commit v6 on v5

--- a/solution.py
+++ b/solution.py
@@ -72,16 +72,10 @@
     return jnp.concatenate([hi, mid, low], axis=0)
 
 
-def send_parts(parts, recv, sems, axis, fill=None):
-    copies = []
-    for i in range(len(STEPS[axis])):
-        d = partner(axis, i)
-        if fill is not None:
-            fill(d)
-        copies.append(send(parts.at[d], recv.at[i], sems, i, axis))
-    if fill is not None:
-        fill(lax.axis_index(axis))
-    return copies
+def send_parts(parts, recv, sems, axis):
+    return [
+        send(parts.at[partner(axis, i)], recv.at[i], sems, i, axis) for i in range(len(STEPS[axis]))
+    ]
 
 
 def sum_parts(parts, recv, copies, axis):
@@ -137,13 +131,12 @@
 def gradient_kernel(
     n_line, n_out, inj_hbm, sf_hbm, of_hbm, lim_hbm, line_hbm, list_ref, count_ref, out_ref,
     inj, sf, of, lim, line, parts, recv_o, slots_o, hot, picked, recv_l, slots_l,
-    wide_of, square, low, high, fall, dsum, qsum, turned, rsum, act,
+    wide_of, square, low, high, fall, dsum, qsum, turned, act,
     rev, recv_r, terms, recv_t, slots_g, slots_f,
     s_in, s_ro, s_go, s_rl, s_rr, s_rt, s_gg, s_gf,
 ):
     n_k = n_line * LB
     n_tiles = n_k // TILE
-    n_sub = TILE // 8
     me_line = lax.axis_index("line")
     me_out = lax.axis_index("out")
     loads = [
@@ -171,10 +164,9 @@
 
     loads[0].wait()
     loads[1].wait()
+    partial = lax.dot_general(inj[...], sf[...], (((1,), (1,)), ((), ())), preferred_element_type=F32)
     for d in range(n_out):
-        parts[d] = lax.dot_general(
-            inj[...], sf[d * LB : (d + 1) * LB, :], (((1,), (1,)), ((), ())), preferred_element_type=F32
-        )
+        parts[d] = partial[:, d * LB : (d + 1) * LB]
     pl.semaphore_wait(barrier, n_out + n_line - 2)
     sent = send_parts(parts, recv_o, s_ro, "out")
     for load in loads[2:]:
@@ -183,13 +175,16 @@
     widen(0, n_tiles // 2)
     slots_o[me_out] = sum_parts(parts, recv_o, sent, "out")
     sent += spread(slots_o, s_go, "out", lambda: widen(n_tiles // 2, n_tiles))
-    flow = jnp.concatenate([slots_o[i] for i in range(n_out)], axis=1)
-    got = add3(jnp.dot(split3(flow), hot[...], preferred_element_type=F32))
-    for i in range(n_line):
-        picked[i] = got[:, i * LB : (i + 1) * LB]
+    flow = split3(jnp.concatenate([slots_o[i] for i in range(n_out)], axis=1))
     falls = [[message(picked, recv_l, s_rl, m, i, FALL_PIECES[m]) for i in range(n_line - 1)] for m in range(3)]
-    for piece in falls:
-        for copy in piece:
+    for m in range(3):
+        first, many = FALL_PIECES[m]
+        got = add3(
+            jnp.dot(flow, hot[:, first * LB : (first + many) * LB], preferred_element_type=F32)
+        )
+        for i in range(many):
+            picked[first + i] = got[:, i * LB : (i + 1) * LB]
+        for copy in falls[m]:
             copy.start()
     for t in range(n_out):
         cols = slice(t * LB, (t + 1) * LB)
@@ -215,38 +210,44 @@
             slots_l[b] = total
             turned[b * LB : (b + 1) * LB, 0:CASES] = total.T
 
-    lanes = lax.broadcasted_iota(jnp.int32, (TILE, LB), 1)
-
-    def tile_step(tile, _):
-        k0 = pl.multiple_of(tile * TILE, TILE)
-        rows = pl.ds(k0, TILE)
-        on = act[pl.ds(tile, 1), :]
-        pair = slots_l[tile // 2]
-        mine = jnp.where(lax.rem(tile, 2) == 0, pair[:, :TILE], pair[:, TILE:]) * on[:, :TILE]
+    lanes = lax.broadcasted_iota(jnp.int32, (LB, LB), 1)
+    n_sub = LB // 8
+
+    def terms_of_block(b):
+        k0 = pl.multiple_of(b * LB, LB)
+        rows = pl.ds(k0, LB)
+        on_a = act[pl.ds(2 * b, 1), :]
+        on_b = act[pl.ds(2 * b + 1, 1), :]
+        on = jnp.concatenate([jnp.broadcast_to(on_a, (TILE, LB)), jnp.broadcast_to(on_b, (TILE, LB))], axis=0)
+        mine = slots_l[b] * jnp.where(lanes[0:1] < TILE, on_a, on_b)
         qsum[...] += add3(jnp.dot(split3(mine), of[rows, :], preferred_element_type=F32))
         masked = turned[rows, :] * on
         for c in range(CASES):
-            fall[c] = jnp.broadcast_to(masked[:, c : c + 1], (TILE, LB))
+            fall[c] = jnp.broadcast_to(masked[:, c : c + 1], (LB, LB))
 
         def reduce_rows(c, sums):
             return jnp.where(lanes == c, jnp.sum(fall[jnp.maximum(c, 0)], axis=1, keepdims=True), sums)
 
         def case_step(c):
-            ffs = fall[c]
-            acc = ffs * square[rows, :]
+            ffs = [fall[c, 8 * i : 8 * i + 8, :] for i in range(n_sub)]
+            acc = [ffs[i] * square[pl.ds(k0 + 8 * i, 8), :] for i in range(n_sub)]
             for t in range(n_out):
                 cols = slice(t * LB, (t + 1) * LB)
-                lo = jnp.concatenate([low[c, :, cols]] * n_sub, axis=0)
-                hi = jnp.concatenate([high[c, :, cols]] * n_sub, axis=0)
-                o = wide_of[rows, cols]
-                q = jnp.minimum(jnp.maximum(ffs * o, lo), hi)
-                acc = acc - q * o
-                size = TILE // 2
-                while size >= 8:
-                    q = q[:size] + q[size:]
-                    size //= 2
-                dsum[c, :, cols] += q
-            fall[c] = acc
+                lo = low[c, :, cols]
+                hi = high[c, :, cols]
+                total = None
+                for i in range(0, n_sub, 2):
+                    pair = []
+                    for j in (i, i + 1):
+                        o = wide_of[pl.ds(k0 + 8 * j, 8), cols]
+                        q = jnp.minimum(jnp.maximum(ffs[j] * o, lo), hi)
+                        acc[j] = acc[j] - q * o
+                        pair.append(q)
+                    both = pair[0] + pair[1]
+                    total = both if total is None else total + both
+                dsum[c, :, cols] += total
+            for i in range(n_sub):
+                fall[c, 8 * i : 8 * i + 8, :] = acc[i]
 
         def group_step(g, sums):
             for e in range(GROUP):
@@ -255,11 +256,10 @@
                 case_step(g * GROUP + e)
             return sums
 
-        sums = lax.fori_loop(0, CASES // GROUP, group_step, jnp.zeros((TILE, LB), F32))
+        sums = lax.fori_loop(0, CASES // GROUP, group_step, jnp.zeros((LB, LB), F32))
         for e in range(GROUP):
             sums = reduce_rows(CASES - GROUP + e, sums)
-        rsum[rows, :] = sums * on
-        return 0
+        rev[b] = (sums * on).T[:CASES]
 
     turns = [[message(rev, recv_r, s_rr, m, i, TERM_PIECES[m]) for i in range(n_line - 1)] for m in range(3)]
 
@@ -270,8 +270,7 @@
             def _():
                 take_falls(m)
 
-        lax.fori_loop(b * (LB // TILE), (b + 1) * (LB // TILE), tile_step, 0)
-        rev[b] = rsum[pl.ds(pl.multiple_of(b * LB, LB), LB), :].T[:CASES]
+        terms_of_block(b)
         for m in range(3):
 
             @pl.when(b == sum(TERM_PIECES[m]) - 1)
@@ -301,19 +300,16 @@
             blocks.append(total)
         return blocks
 
-    def placed(three, d, cols):
-        table = hot[pl.ds(pl.multiple_of(d * LB, LB), LB), cols]
-        return add3(lax.dot_general(three, table, (((1,), (1,)), ((), ())), preferred_element_type=F32))
-
-    early = split3(jnp.concatenate(summed(0) + summed(1), axis=1))
-    for t in range(n_out):
-        terms[t] += placed(early, t, slice(0, n_k - LB))
-    late = split3(summed(2)[0])
-
-    def fill(d):
-        terms[d] += placed(late, d, slice(n_k - LB, n_k))
-
-    scattered = send_parts(terms, recv_t, s_rt, "out", fill)
+    def place(three, cols):
+        got = add3(
+            lax.dot_general(three, hot[:, cols], (((1,), (1,)), ((), ())), preferred_element_type=F32)
+        )
+        for t in range(n_out):
+            terms[t] += got[:, t * LB : (t + 1) * LB]
+
+    place(split3(jnp.concatenate(summed(0) + summed(1), axis=1)), slice(0, n_k - LB))
+    place(split3(summed(2)[0]), slice(n_k - LB, n_k))
+    scattered = send_parts(terms, recv_t, s_rt, "out")
     grad = sum_parts(terms, recv_t, scattered, "out")
     slots_g[me_out] = (grad * (2.0 / NO)).astype(BF16)
     sent += scattered + spread(slots_g, s_gg, "out")
@@ -363,10 +359,9 @@
             pltpu.VMEM((n_k, LB), F32),
             pltpu.VMEM((CASES, 8, n_l), F32),
             pltpu.VMEM((CASES, 8, n_l), F32),
-            pltpu.VMEM((CASES, TILE, LB), F32),
+            pltpu.VMEM((CASES, LB, LB), F32),
             pltpu.VMEM((CASES, 8, n_l), F32),
             pltpu.VMEM((CASES, n_l), F32),
-            pltpu.VMEM((n_k, LB), F32),
             pltpu.VMEM((n_k, LB), F32),
             pltpu.VMEM((n_k // TILE, LB), F32),
             per_line,

time: 123 us -> 118 us (0.959)
  Pallas kernels: 119 us -> 115 us
    pallas_call x1, Pallas kernels: 119 us -> 115 us  [shards(): pl.pallas_call(functools.partial(gradient_kernel, n_line, n_out), in_spec...]
where the time goes in v6:
time: 118 us; the launch traced here: 117 us
  Pallas kernels  115 us (97%)
  local copies, waits for them, and re-layouts  1.47 us (1%)
    pallas_call x1, Pallas kernels, shards(): pl.pallas_call(functools.partial(gradient_kernel, n_line, n_out), in_spec...  115 us

profile of v6, /device:TPU:0, one launch (start us, length us, event | category | flops | bytes accessed | tf_op | source)
XLA Modules:
  0.0 117.3 jit_solution(15862034166586702142)
XLA Ops:
  0.7 115.2 %gradient.1 = f32[32,512]{1,0:T(8,128)} custom-call(bf16[32,512]{1,0:T(8,128)(2,1)} %inj_hbm.1, bf16[2048,512]{1,0:T(8,128)(2,1)} %sf_hbm.1, bf16[1024,2048]{1,0:T(8,128)(2,1)} %of_hbm.1, f32[1,2048]{1,0:T(1,128)} %bitcast.4, s32[1,1024]{1,0:T(1,128)} %bitcast.5, s32[1,16]{1,0:T(1,128)} %list_ref.1, s32[1,1]{1,0:T(1,128)} %bitcast.3.count_ref), custom_call_target="tpu_custom_call" | custom-call | tf_op jit(solution)/shard_map/gradient/pallas_call | solution.py:340
  115.8 1.5 %copy.10 = f32[32,512]{1,0:T(8,128)} copy(f32[32,512]{1,0:T(8,128)} %gradient.1) | data formatting | bytes 131072

commit v7 on v6

--- a/solution.py
+++ b/solution.py
@@ -131,7 +131,7 @@
 def gradient_kernel(
     n_line, n_out, inj_hbm, sf_hbm, of_hbm, lim_hbm, line_hbm, list_ref, count_ref, out_ref,
     inj, sf, of, lim, line, parts, recv_o, slots_o, hot, picked, recv_l, slots_l,
-    wide_of, square, low, high, fall, dsum, qsum, turned, act,
+    wide_of, square, low, high, fall, dsum, turned, act,
     rev, recv_r, terms, recv_t, slots_g, slots_f,
     s_in, s_ro, s_go, s_rl, s_rr, s_rt, s_gg, s_gf,
 ):
@@ -145,9 +145,9 @@
             [(inj_hbm, inj), (sf_hbm, sf), (line_hbm, line), (lim_hbm, lim), (of_hbm, of)]
         )
     ]
-    for load in loads:
+    barrier = greet()
+    for load in loads[:4]:
         load.start()
-    barrier = greet()
 
     def widen(first, last):
         def one(tile, _):
@@ -164,6 +164,7 @@
 
     loads[0].wait()
     loads[1].wait()
+    loads[4].start()
     partial = lax.dot_general(inj[...], sf[...], (((1,), (1,)), ((), ())), preferred_element_type=F32)
     for d in range(n_out):
         parts[d] = partial[:, d * LB : (d + 1) * LB]
@@ -172,9 +173,9 @@
     for load in loads[2:]:
         load.wait()
     hot_table(hot, line, n_out, n_k)
-    widen(0, n_tiles // 2)
+    widen(0, n_tiles // 2 - 1)
     slots_o[me_out] = sum_parts(parts, recv_o, sent, "out")
-    sent += spread(slots_o, s_go, "out", lambda: widen(n_tiles // 2, n_tiles))
+    sent += spread(slots_o, s_go, "out", lambda: widen(n_tiles // 2 - 1, n_tiles))
     flow = split3(jnp.concatenate([slots_o[i] for i in range(n_out)], axis=1))
     falls = [[message(picked, recv_l, s_rl, m, i, FALL_PIECES[m]) for i in range(n_line - 1)] for m in range(3)]
     for m in range(3):
@@ -192,7 +193,6 @@
             low[c, :, cols] = jnp.broadcast_to(-lim[:, cols] - slots_o[t, c : c + 1, :], (8, LB))
             high[c, :, cols] = jnp.broadcast_to(lim[:, cols] - slots_o[t, c : c + 1, :], (8, LB))
     dsum[...] = jnp.zeros_like(dsum)
-    qsum[...] = jnp.zeros_like(qsum)
     ids = lax.broadcasted_iota(jnp.int32, (n_tiles, n_tiles), 0)
     place = lax.broadcasted_iota(jnp.int32, (n_tiles, n_tiles), 1)
     listed = (list_ref[...] == ids) & (place < count_ref[...])
@@ -219,8 +219,6 @@
         on_a = act[pl.ds(2 * b, 1), :]
         on_b = act[pl.ds(2 * b + 1, 1), :]
         on = jnp.concatenate([jnp.broadcast_to(on_a, (TILE, LB)), jnp.broadcast_to(on_b, (TILE, LB))], axis=0)
-        mine = slots_l[b] * jnp.where(lanes[0:1] < TILE, on_a, on_b)
-        qsum[...] += add3(jnp.dot(split3(mine), of[rows, :], preferred_element_type=F32))
         masked = turned[rows, :] * on
         for c in range(CASES):
             fall[c] = jnp.broadcast_to(masked[:, c : c + 1], (LB, LB))
@@ -282,6 +280,11 @@
 
     lax.fori_loop(0, n_line, block_step, 0)
 
+    falling = []
+    for b in range(n_line):
+        on = jnp.where(lanes[0:1] < TILE, act[2 * b : 2 * b + 1, :], act[2 * b + 1 : 2 * b + 2, :])
+        falling.append(slots_l[b] * on)
+    qsum = add3(jnp.dot(split3(jnp.concatenate(falling, axis=1)), of[...], preferred_element_type=F32))
     idle = TILE * (n_tiles - jnp.sum(act[...], axis=0, keepdims=True))
     for t in range(n_out):
         cols = slice(t * LB, (t + 1) * LB)
@@ -361,7 +364,6 @@
             pltpu.VMEM((CASES, 8, n_l), F32),
             pltpu.VMEM((CASES, LB, LB), F32),
             pltpu.VMEM((CASES, 8, n_l), F32),
-            pltpu.VMEM((CASES, n_l), F32),
             pltpu.VMEM((n_k, LB), F32),
             pltpu.VMEM((n_k // TILE, LB), F32),
             per_line,

time: 118 us -> 117 us (level)
  no operation moved by 1% of the time
where the time goes in v7:
time: 117 us
  Pallas kernels  115 us (98%)
  local copies, waits for them, and re-layouts  1.47 us (1%)
    pallas_call x1, Pallas kernels, shards(): pl.pallas_call(functools.partial(gradient_kernel, n_line, n_out), in_spec...  115 us

profile of v7, /device:TPU:0, one launch (start us, length us, event | category | flops | bytes accessed | tf_op | source)
XLA Modules:
  0.0 116.8 jit_solution(4327471006735773399)
XLA Ops:
  0.7 114.7 %gradient.1 = f32[32,512]{1,0:T(8,128)} custom-call(bf16[32,512]{1,0:T(8,128)(2,1)} %inj_hbm.1, bf16[2048,512]{1,0:T(8,128)(2,1)} %sf_hbm.1, bf16[1024,2048]{1,0:T(8,128)(2,1)} %of_hbm.1, f32[1,2048]{1,0:T(1,128)} %bitcast.4, s32[1,1024]{1,0:T(1,128)} %bitcast.5, s32[1,16]{1,0:T(1,128)} %list_ref.1, s32[1,1]{1,0:T(1,128)} %bitcast.3.count_ref), custom_call_target="tpu_custom_call" | custom-call | tf_op jit(solution)/shard_map/gradient/pallas_call | solution.py:343
  115.3 1.5 %copy.10 = f32[32,512]{1,0:T(8,128)} copy(f32[32,512]{1,0:T(8,128)} %gradient.1) | data formatting | bytes 131072

commit v8 on v7

--- a/solution.py
+++ b/solution.py
@@ -139,14 +139,22 @@
     n_tiles = n_k // TILE
     me_line = lax.axis_index("line")
     me_out = lax.axis_index("out")
+    n_half = n_out * LB // 2
     loads = [
         pltpu.make_async_copy(src, dst, s_in.at[i])
         for i, (src, dst) in enumerate(
-            [(inj_hbm, inj), (sf_hbm, sf), (line_hbm, line), (lim_hbm, lim), (of_hbm, of)]
+            [
+                (inj_hbm, inj),
+                (sf_hbm.at[pl.ds(0, n_half)], sf.at[pl.ds(0, n_half)]),
+                (sf_hbm.at[pl.ds(n_half, n_half)], sf.at[pl.ds(n_half, n_half)]),
+                (line_hbm, line),
+                (lim_hbm, lim),
+                (of_hbm, of),
+            ]
         )
     ]
     barrier = greet()
-    for load in loads[:4]:
+    for load in loads[:5]:
         load.start()
 
     def widen(first, last):
@@ -163,14 +171,19 @@
         lax.fori_loop(first, last, one, 0)
 
     loads[0].wait()
-    loads[1].wait()
-    loads[4].start()
-    partial = lax.dot_general(inj[...], sf[...], (((1,), (1,)), ((), ())), preferred_element_type=F32)
-    for d in range(n_out):
-        parts[d] = partial[:, d * LB : (d + 1) * LB]
+    for h in range(2):
+        loads[1 + h].wait()
+        if h == 1:
+            loads[5].start()
+        partial = lax.dot_general(
+            inj[...], sf[h * n_half : (h + 1) * n_half, :], (((1,), (1,)), ((), ())),
+            preferred_element_type=F32,
+        )
+        for d in range(n_out // 2):
+            parts[h * (n_out // 2) + d] = partial[:, d * LB : (d + 1) * LB]
     pl.semaphore_wait(barrier, n_out + n_line - 2)
     sent = send_parts(parts, recv_o, s_ro, "out")
-    for load in loads[2:]:
+    for load in loads[3:]:
         load.wait()
     hot_table(hot, line, n_out, n_k)
     widen(0, n_tiles // 2 - 1)
@@ -372,7 +385,7 @@
             per_out,
             pltpu.VMEM((n_out,) + block, BF16),
             pltpu.VMEM((n_line, CASES, shift_factors.shape[1]), BF16),
-            dma((5,)),
+            dma((6,)),
             dma((2, n_out)),
             dma((2, n_out)),
             dma((2, 3, n_line)),

time: 117 us -> 121 us (1.034)
  Pallas kernels: 115 us -> 118 us
    pallas_call x1, Pallas kernels: 115 us -> 118 us  [shards(): pl.pallas_call(functools.partial(gradient_kernel, n_line, n_out), in_spec...]
where the time goes in v8:
time: 121 us; the launch traced here: 120 us
  Pallas kernels  118 us (98%)
  local copies, waits for them, and re-layouts  1.47 us (1%)
    pallas_call x1, Pallas kernels, shards(): pl.pallas_call(functools.partial(gradient_kernel, n_line, n_out), in_spec...  118 us

profile of v8, /device:TPU:0, one launch (start us, length us, event | category | flops | bytes accessed | tf_op | source)
XLA Modules:
  0.0 120.0 jit_solution(12084365083794813822)
XLA Ops:
  0.7 117.9 %gradient.1 = f32[32,512]{1,0:T(8,128)} custom-call(bf16[32,512]{1,0:T(8,128)(2,1)} %inj_hbm.1, bf16[2048,512]{1,0:T(8,128)(2,1)} %sf_hbm.1, bf16[1024,2048]{1,0:T(8,128)(2,1)} %of_hbm.1, f32[1,2048]{1,0:T(1,128)} %bitcast.4, s32[1,1024]{1,0:T(1,128)} %bitcast.5, s32[1,16]{1,0:T(1,128)} %list_ref.1, s32[1,1]{1,0:T(1,128)} %bitcast.3.count_ref), custom_call_target="tpu_custom_call" | custom-call | tf_op jit(solution)/shard_map/gradient/pallas_call | solution.py:356
  118.5 1.5 %copy.10 = f32[32,512]{1,0:T(8,128)} copy(f32[32,512]{1,0:T(8,128)} %gradient.1) | data formatting | bytes 131072
